TPU v7x, 512 devices: a whole 4x8x8 slice. The times are simulated.
512 devices in a mesh: member: 16 (over y, core), dom: 32 (over z, x).
Axes of the slice: x: 4, y: 8, z: 8, core: 2. Of those that a mesh axis runs over, the one named last changes fastest.
Arguments:
- grid_in: bfloat16 [524288, 227], P(('member', 'dom')), parts along dimension 0, may hold values from -6 to 6
- w_embed: bfloat16 [227, 512], replicated, may hold values from -0.375 to 0.375
- w_grid_send: bfloat16 [512, 512], replicated, may hold values from -0.25 to 0.25
- enc_feat: bfloat16 [4, 65536], P(None, 'dom'), may hold values from -6 to 6
- w_enc_edge: bfloat16 [4, 512], replicated, may hold values from -3 to 3
- enc_sender: int32 [65536], P('dom'), may hold values from 0 to 1535, as said below
- enc_offset: int32 [65536], P('dom'), may hold values from -1 to 127, as said below
- grid_rows: int32 [1024, 16], P('dom'), may hold values from 0 to 1023, as said below
- w_proc_send: bfloat16 [2, 512, 512], replicated, may hold values from -0.25 to 0.25
- w_proc_edge: bfloat16 [2, 4, 512], replicated, may hold values from -3 to 3
- w_proc_node: bfloat16 [2, 512, 512], replicated, may hold values from -0.25 to 0.25
- mesh_feat: bfloat16 [4, 32768], P(None, 'dom'), may hold values from -6 to 6
- mesh_sender: int32 [32768], P('dom'), may hold values from 0 to 383, as said below
- mesh_offset: int32 [32768], P('dom'), may hold values from -1 to 127, as said below
- mesh_rows: int32 [1024, 8], P('dom'), may hold values from 0 to 127, as said below
- w_skip: bfloat16 [512, 512], replicated, may hold values from -0.25 to 0.25
- w_dec: bfloat16 [512, 512], replicated, may hold values from -0.25 to 0.25
- w_dec_edge: bfloat16 [4, 512], replicated, may hold values from -3 to 3
- dec_feat: bfloat16 [4, 98304], P(None, 'dom'), may hold values from -6 to 6
- dec_sender: int32 [98304], P('dom'), may hold values from 0 to 383, as said below
- dec_offset: int32 [98304], P('dom'), may hold values from -1 to 127, as said below
- dec_block: int32 [768], P('dom'), may hold values from 0 to 7, as said below
- dec_rows: int32 [1024, 8], P('dom'), may hold values from 0 to 127, as said below
- w_out: bfloat16 [512, 227], replicated, may hold values from -0.25 to 0.25
Outputs:
- forecast: bfloat16 [524288, 227], P(('member', 'dom')), parts along dimension 0
There are 16 independent parts, one for each index of `member`. A program takes and returns all parts, laid end to end along the dimension named above; an argument that names none is the same for every part. Nothing has to cross between parts.
Inputs may be any that keep to these rules, and one draw needn't show every extreme that they name: `enc_sender`: an entry below 1024 is a grid row of the device that holds the edge; an entry 1024 + p * 16 + s names slot s of what device p lends it, never the device itself. `enc_offset`: A mesh row of the holding device; -1 marks a padded edge. `grid_rows`: row d * 32 + p holds the local grid rows of device p that p lends to device d. `mesh_sender`: an entry below 128 is a mesh row of the holding device; an entry 128 + p * 8 + s names slot s of what device p lends it, never the device itself. `mesh_offset`: A mesh row of the holding device; -1 marks a padded edge. `mesh_rows`: row d * 32 + p holds the local mesh rows of device p that p lends to device d. `dec_sender`: an entry below 128 is a mesh row of the holding device; an entry 128 + p * 8 + s names slot s of what device p lends it, never the device itself. `dec_offset`: A row inside the 128-row grid block named by dec_block; -1 marks a padded edge. `dec_block`: A 128-row block of the holding device's grid rows. `dec_rows`: row d * 32 + p holds the local mesh rows of device p that p lends to device d.
All inputs are finite; a program needn't handle non-finite values.
Results may differ from a plain program's by a relative error of at most 0.012.
Values may be sent and summed in bfloat16 or wider, within the bound.
A program may use at most 64 MiB of HBM per device.

v0:
```python
import jax
import jax.numpy as jnp
from jax import lax
from jax.sharding import PartitionSpec as P

M_DEV = 128
LAYERS = 2


def edge_messages(picked, features, w_edge):
    edge_term = lax.dot_general(
        features, w_edge, (((0,), (0,)), ((), ())), preferred_element_type=jnp.float32
    )
    return jax.nn.silu(picked.astype(jnp.float32) + edge_term).astype(jnp.bfloat16)


def mean_local(messages, targets, n_rows):
    onehot = targets[None, :] == jnp.arange(n_rows, dtype=jnp.int32)[:, None]
    summed = jnp.dot(onehot.astype(jnp.bfloat16), messages, preferred_element_type=jnp.float32)
    counted = jnp.sum(onehot, axis=1).astype(jnp.float32)
    return (summed / jnp.maximum(counted, 1.0)[:, None]).astype(jnp.bfloat16)


def mean_blocked(messages, targets, block_ids, n_blocks):
    edge_blocks = targets.shape[0] // 128
    onehot = targets.reshape(edge_blocks, 1, 128) == jnp.arange(128, dtype=jnp.int32).reshape(
        1, 128, 1
    )
    block_sums = jnp.einsum(
        "brj,bjd->brd",
        onehot.astype(jnp.bfloat16),
        messages.reshape(edge_blocks, 128, -1),
        preferred_element_type=jnp.float32,
    )
    block_counts = jnp.sum(onehot, axis=2).astype(jnp.float32)
    select = (block_ids[None, :] == jnp.arange(n_blocks, dtype=jnp.int32)[:, None]).astype(
        jnp.float32
    )
    summed = jnp.einsum("rb,bjd->rjd", select, block_sums, precision=lax.Precision.HIGHEST)
    counted = jnp.dot(select, block_counts, precision=lax.Precision.HIGHEST)
    averaged = summed / jnp.maximum(counted, 1.0)[:, :, None]
    return averaged.reshape(n_blocks * 128, -1).astype(jnp.bfloat16)


def local(
    grid_in,
    w_embed,
    w_grid_send,
    enc_feat,
    w_enc_edge,
    enc_sender,
    enc_offset,
    grid_rows,
    w_proc_send,
    w_proc_edge,
    w_proc_node,
    mesh_feat,
    mesh_sender,
    mesh_offset,
    mesh_rows,
    w_skip,
    w_dec,
    w_dec_edge,
    dec_feat,
    dec_sender,
    dec_offset,
    dec_block,
    dec_rows,
    w_out,
):
    width = w_embed.shape[1]
    n_grid = grid_in.shape[0]
    n_mesh = M_DEV
    grid_latent = jax.nn.silu(jnp.dot(grid_in, w_embed, preferred_element_type=jnp.float32)).astype(
        jnp.bfloat16
    )
    grid_send = jnp.dot(grid_latent, w_grid_send, preferred_element_type=jnp.float32).astype(
        jnp.bfloat16
    )
    grid_lists = lax.all_to_all(grid_rows, "dom", split_axis=0, concat_axis=0, tiled=True)
    grid_incoming = lax.all_to_all(
        jnp.take(grid_send, grid_lists, axis=0), "dom", split_axis=0, concat_axis=0, tiled=True
    )
    grid_table = jnp.concatenate([grid_send, grid_incoming.reshape(-1, width)], axis=0)
    messages = edge_messages(jnp.take(grid_table, enc_sender, axis=0), enc_feat, w_enc_edge)
    mesh_latent = mean_local(messages, enc_offset, n_mesh)
    own_index = lax.axis_index("dom")

    def global_rows(senders, lent):
        slots = lent.shape[1]
        shifted = jnp.maximum(senders - n_mesh, 0)
        peer_index = shifted // slots
        slot_index = shifted % slots
        listed = lent[peer_index, slot_index]
        return jnp.where(
            senders >= n_mesh, peer_index * n_mesh + listed, own_index * n_mesh + senders
        )

    mesh_index = global_rows(mesh_sender, mesh_rows)
    dec_index = global_rows(dec_sender, dec_rows)

    def spread(values, index):
        whole_mesh = lax.all_gather(values, "dom", axis=0, tiled=True)
        return jnp.take(whole_mesh, index, axis=0)

    for layer_index in range(LAYERS):
        mesh_send = jnp.dot(
            mesh_latent, w_proc_send[layer_index], preferred_element_type=jnp.float32
        ).astype(jnp.bfloat16)
        messages = edge_messages(spread(mesh_send, mesh_index), mesh_feat, w_proc_edge[layer_index])
        mesh_mean = mean_local(messages, mesh_offset, n_mesh)
        update = jax.nn.silu(
            jnp.dot(mesh_mean, w_proc_node[layer_index], preferred_element_type=jnp.float32)
        )
        mesh_latent = (mesh_latent.astype(jnp.float32) + update).astype(jnp.bfloat16)
    messages = edge_messages(spread(mesh_latent, dec_index), dec_feat, w_dec_edge)
    grid_mean = mean_blocked(messages, dec_offset, dec_block, n_grid // 128)
    mixed = jnp.dot(grid_mean, w_dec, preferred_element_type=jnp.float32) + jnp.dot(
        grid_latent, w_skip, preferred_element_type=jnp.float32
    )
    hidden = jax.nn.silu(mixed).astype(jnp.bfloat16)
    return jnp.dot(hidden, w_out, preferred_element_type=jnp.float32).astype(jnp.bfloat16)


def solution(mesh):
    in_specs = (
        P(("member", "dom"), None),
        P(),
        P(),
        P(None, "dom"),
        P(),
        P("dom"),
        P("dom"),
        P("dom", None),
        P(),
        P(),
        P(),
        P(None, "dom"),
        P("dom"),
        P("dom"),
        P("dom", None),
        P(),
        P(),
        P(),
        P(None, "dom"),
        P("dom"),
        P("dom"),
        P("dom"),
        P("dom", None),
        P(),
    )
    out_specs = P(("member", "dom"), None)
    return jax.shard_map(local, mesh=mesh, in_specs=in_specs, out_specs=out_specs, check_vma=False)
```

profile of v0, /device:TPU:56, one launch (start us, length us, event | category | flops | bytes accessed | tf_op | source)
XLA Modules:
  0.0 382.2 jit_solution(15282356685777274387)
XLA Ops:
  6.5 1.4 copy.35
  8.0 13.2 %all-to-all-start = ((s32[32,1,16]{2,1,0:T(1,128)}), s32[32,1,16]{2,1,0:T(1,128)S(1)}, u32[]{:S(2)}, u32[]{:S(2)}) async-start(s32[32,1,16]{2,1,0:T(1,128)} %bitcast.2), calls=%async_computation | async-start | bytes 32768 | tf_op jit(solution)/shard_map/all_to_all | solution.py:80
  21.1 1.9 multiply_convert_fusion.5
  24.8 6.0 %all-to-all-done = s32[32,1,16]{2,1,0:T(1,128)S(1)} async-done(((s32[32,1,16]{2,1,0:T(1,128)}), s32[32,1,16]{2,1,0:T(1,128)S(1)}, u32[]{:S(2)}, u32[]{:S(2)}) %all-to-all-start) | async-done | bytes 2080 | tf_op jit(solution)/shard_map/all_to_all | solution.py:80
  30.9 2.0 gather_fusion.1
  33.9 3.9 %all-to-all-start.1 = ((bf16[32,16,512]{2,1,0:T(8,128)(2,1)}), bf16[32,16,512]{2,1,0:T(8,128)(2,1)S(1)}, u32[]{:S(2)}, u32[]{:S(2)}) async-start(bf16[32,16,512]{2,1,0:T(8,128)(2,1)} %broadcast_select_fusion), calls=%async_computation.1 | async-start | bytes 1048576 | tf_op jit(solution)/shard_map/all_to_all | solution.py:81
  38.1 16.9 %all-to-all-done.1 = bf16[32,16,512]{2,1,0:T(8,128)(2,1)S(1)} async-done(((bf16[32,16,512]{2,1,0:T(8,128)(2,1)}), bf16[32,16,512]{2,1,0:T(8,128)(2,1)S(1)}, u32[]{:S(2)}, u32[]{:S(2)}) %all-to-all-start.1) | async-done | bytes 524320 | tf_op jit(solution)/shard_map/all_to_all | solution.py:81
  55.8 1.1 pad_maximum_fusion
  56.9 9.2 %gather_fusion.2 = bf16[2048,512]{1,0:T(8,128)(2,1)} fusion(bf16[1536,512]{1,0:T(8,128)(2,1)S(1)} %pad_maximum_fusion, s32[2048]{0:T(1024)S(1)} %fusion.51), kind=kCustom, calls=%fused_computation.4 | custom fusion | bytes 4202496 | tf_op jit(solution)/shard_map/jit(_take)/gather | solution.py:85
  66.1 3.6 fusion.11
  70.8 4.7 %gather_fusion.3 = s32[1024]{0:T(1024)S(1)} fusion(s32[32,8]{0,1:T(8,128)S(1)} %copy-done.2, s32[1024]{0:T(1024)S(1)} %fusion.54), kind=kCustom, calls=%fused_computation.5 | custom fusion | bytes 16384 | tf_op jit(solution)/shard_map/gather | solution.py:94
  75.8 79.0 %all-gather.4.cloned.1.call-done = bf16[4096,512]{1,0:T(8,128)(2,1)} async-done(((bf16[128,512]{1,0:T(8,128)(2,1)}), bf16[4096,512]{1,0:T(8,128)(2,1)}) %all-gather.4.cloned.1.call-update) | async-done | bytes 4194320 | tf_op jit(solution)/shard_map/all_gather | solution.py:103
  154.8 6.7 %gather_fusion.5 = bf16[1024,512]{1,0:T(8,128)(2,1)S(1)} fusion(bf16[4096,512]{1,0:T(8,128)(2,1)} %all-gather.4.cloned.1.call-done, s32[1024]{0:T(1024)S(1)} %broadcast_clamp_fusion.1), kind=kCustom, calls=%fused_computation.clone | custom fusion | bytes 2101248 | tf_op jit(solution)/shard_map/jit(_take)/gather | solution.py:104
  161.5 1.1 fusion.15
  162.6 1.3 add_convert_fusion.1
  165.1 84.7 %all-gather.6.cloned.1.call-done = bf16[4096,512]{1,0:T(8,128)(2,1)} async-done(((bf16[128,512]{1,0:T(8,128)(2,1)}), bf16[4096,512]{1,0:T(8,128)(2,1)}) %all-gather.6.cloned.1.call-update) | async-done | bytes 4194320 | tf_op jit(solution)/shard_map/all_gather | solution.py:103
  249.8 6.7 %gather_fusion.6 = bf16[1024,512]{1,0:T(8,128)(2,1)S(1)} fusion(bf16[4096,512]{1,0:T(8,128)(2,1)} %all-gather.6.cloned.1.call-done, s32[1024]{0:T(1024)S(1)} %broadcast_clamp_fusion.1), kind=kCustom, calls=%fused_computation.1.clone | custom fusion | bytes 2101248 | tf_op jit(solution)/shard_map/jit(_take)/gather | solution.py:104
  256.5 1.1 fusion.13
  259.5 13.2 %gather_fusion = s32[3072]{0:T(1024)S(1)} fusion(s32[32,8]{0,1:T(8,128)S(1)} %copy-done.1, s32[3072]{0:T(1024)S(1)} %fusion.46), kind=kCustom, calls=%fused_computation.2 | custom fusion | bytes 49152 | tf_op jit(solution)/shard_map/gather | solution.py:94
  272.8 70.9 %all-gather.8.cloned.1.call-done = bf16[4096,512]{1,0:T(8,128)(2,1)} async-done(((bf16[128,512]{1,0:T(8,128)(2,1)}), bf16[4096,512]{1,0:T(8,128)(2,1)}) %all-gather.8.cloned.1.call-update) | async-done | bytes 4194320 | tf_op jit(solution)/shard_map/all_gather | solution.py:103
  343.6 16.0 %gather_fusion.4 = bf16[3072,512]{1,0:T(8,128)(2,1)} fusion(bf16[4096,512]{1,0:T(8,128)(2,1)} %all-gather.8.cloned.1.call-done, s32[3072]{0:T(1024)S(1)} %broadcast_clamp_fusion), kind=kCustom, calls=%fused_computation.6 | custom fusion | bytes 6303744 | tf_op jit(solution)/shard_map/jit(_take)/gather | solution.py:104
  359.7 4.2 %multiply_convert_fusion = bf16[3072,512]{1,0:T(8,128)(2,1)S(1)} fusion(bf16[4,3072]{1,0:T(4,128)(2,1)S(1)} %copy-done.16, bf16[4,512]{1,0:T(4,128)(2,1)S(1)} %copy-done.21, bf16[3072,512]{1,0:T(8,128)(2,1)} %gather_fusion.4, pred[3072]{0:T(1024)(128)(4,1)S(1)} %get-tuple-element.6), kind=kOutput, calls=%fused_computation.9 | convolution fusion | flops 25165824 | bytes 6323200 | tf_op jit(solution)/shard_map/dot_general | solution.py:11
  364.9 5.8 %divide_convert_fusion = bf16[8,128,512]{2,0,1:T(8,128)(2,1)S(1)} fusion(f32[24,128,512]{2,1,0:T(8,128)S(1)} %fusion.2, f32[8,128]{0,1:T(8,128)S(1)} %copy.37, s32[24]{0:T(128)S(1)} %copy-done.11), kind=kOutput, calls=%fused_computation.12 | convolution fusion | flops 152043712 | bytes 7344224 | tf_op jit(solution)/shard_map/rb,bjd->rjd/dot_general | solution.py:39
  372.4 3.3 fusion.7
  (79 shorter events, 10.7 us)
Async XLA Ops:
  6.5 17.6 %copy-start = (bf16[512,512]{1,0:T(8,128)(2,1)S(1)}, bf16[512,512]{1,0:T(8,128)(2,1)}, u32[]{:S(2)}) copy-start(bf16[512,512]{1,0:T(8,128)(2,1)} %param.28) | copy-start | bytes 1572868
  8.0 22.8 %all-to-all-start = ((s32[32,1,16]{2,1,0:T(1,128)}), s32[32,1,16]{2,1,0:T(1,128)S(1)}, u32[]{:S(2)}, u32[]{:S(2)}) async-start(s32[32,1,16]{2,1,0:T(1,128)} %bitcast.2), calls=%async_computation | async-start | bytes 32768 | tf_op jit(solution)/shard_map/all_to_all | solution.py:80
  23.0 1.1 copy-start.22
  32.9 4.9 %copy-start.9 = (s32[2048]{0:T(1024)S(1)}, s32[2048]{0:T(1024)}, u32[]{:S(2)}) copy-start(s32[2048]{0:T(1024)} %param.32) | copy-start | bytes 24580
  32.9 5.1 %copy-start.7 = (s32[2048]{0:T(1024)S(1)}, s32[2048]{0:T(1024)}, u32[]{:S(2)}) copy-start(s32[2048]{0:T(1024)} %param.31) | copy-start | bytes 24580
  33.9 21.1 %all-to-all-start.1 = ((bf16[32,16,512]{2,1,0:T(8,128)(2,1)}), bf16[32,16,512]{2,1,0:T(8,128)(2,1)S(1)}, u32[]{:S(2)}, u32[]{:S(2)}) async-start(bf16[32,16,512]{2,1,0:T(8,128)(2,1)} %broadcast_select_fusion), calls=%async_computation.1 | async-start | bytes 1048576 | tf_op jit(solution)/shard_map/all_to_all | solution.py:81
  37.8 117.0 %all-gather.4.cloned.1.call-start = ((), (), s32[]{:S(2)}) async-start(), calls=%async_computation.2 | async-start | bytes 4325376 | tf_op jit(solution)/shard_map/all_gather | solution.py:103
  56.9 9.2 %copy-start.17 = (bf16[4,2048]{1,0:T(4,128)(2,1)S(1)}, bf16[4,2048]{1,0:T(4,128)(2,1)}, u32[]{:S(2)}) copy-start(bf16[4,2048]{1,0:T(4,128)(2,1)} %param.29) | copy-start | bytes 49156
  56.9 9.2 %copy-start.20 = (bf16[4,512]{1,0:T(4,128)(2,1)S(1)}, bf16[4,512]{1,0:T(4,128)(2,1)}, u32[]{:S(2)}) copy-start(bf16[4,512]{1,0:T(4,128)(2,1)} %param.30) | copy-start | bytes 12292
  66.1 3.7 copy-start.12
  66.1 4.7 %copy-start.8 = (s32[1024]{0:T(1024)S(1)}, s32[1024]{0:T(1024)}, u32[]{:S(2)}) copy-start(s32[1024]{0:T(1024)} %param.38) | copy-start | bytes 12292
  70.7 179.1 %all-gather.6.cloned.1.call-start = ((), (), s32[]{:S(2)}) async-start(), calls=%async_computation.3 | async-start | bytes 4325376 | tf_op jit(solution)/shard_map/all_gather | solution.py:103
  70.8 4.8 %copy-start.10 = (s32[1024]{0:T(1024)S(1)}, s32[1024]{0:T(1024)}, u32[]{:S(2)}) copy-start(s32[1024]{0:T(1024)} %param.39) | copy-start | bytes 12292
  75.8 85.7 %copy-start.18 = (bf16[4,1024]{1,0:T(4,128)(2,1)S(1)}, bf16[4,1024]{1,0:T(4,128)(2,1)}, u32[]{:S(2)}) copy-start(bf16[4,1024]{1,0:T(4,128)(2,1)} %param.37) | copy-start | bytes 24580
  75.8 85.7 %copy-start.19 = (bf16[2,4,512]{2,1,0:T(4,128)(2,1)S(1)}, bf16[2,4,512]{2,1,0:T(4,128)(2,1)}, u32[]{:S(2)}) copy-start(bf16[2,4,512]{2,1,0:T(4,128)(2,1)} %param.35) | copy-start | bytes 24580
  164.9 178.8 %all-gather.8.cloned.1.call-start = ((), (), s32[]{:S(2)}) async-start(), calls=%async_computation.4 | async-start | bytes 4325376 | tf_op jit(solution)/shard_map/all_gather | solution.py:103
  256.5 1.2 copy-start.13
  257.8 1.5 copy-start.11
  257.8 1.7 copy-start.6
  257.8 1.7 copy-start.1
  272.7 87.0 %copy-start.16 = (bf16[4,3072]{1,0:T(4,128)(2,1)S(1)}, bf16[4,3072]{1,0:T(4,128)(2,1)}, u32[]{:S(2)}) copy-start(bf16[4,3072]{1,0:T(4,128)(2,1)} %param.44) | copy-start | bytes 73732
  272.8 86.9 %copy-start.21 = (bf16[4,512]{1,0:T(4,128)(2,1)S(1)}, bf16[4,512]{1,0:T(4,128)(2,1)}, u32[]{:S(2)}) copy-start(bf16[4,512]{1,0:T(4,128)(2,1)} %param.43) | copy-start | bytes 12292
  371.0 1.4 copy-start.14
  371.0 1.4 copy-start.15
  (4 other events, 3.8 us)
Sparse Core Ops, SparseCore 0:
  70.8 83.9 all-gather.3
  165.0 84.7 all-gather.5
  258.9 84.7 all-gather.7
where the time goes:
time: 383 us; the launch traced here: 382 us
  waiting for transfers between devices  258 us (67%)
  local copies, waits for them, and re-layouts  63.3 us (17%)
  matrix products  27.5 us (7%)
  starting transfers between devices  17.4 us (5%)
  between operations  13.6 us (4%)
    all_gather x3, waiting for transfers between devices, spread(): whole_mesh = lax.all_gather(values, 'dom', axis=0, tiled=True)  235 us
    gather x3, local copies, waits for them, and re-layouts, spread(): return jnp.take(whole_mesh, index, axis=0)  29.5 us
    gather x2, local copies, waits for them, and re-layouts, global_rows(): listed = lent[peer_index, slot_index]  17.9 us
    all_to_all x1, waiting for transfers between devices, local(): lax.all_to_all(jnp.take(grid_send, grid_lists, axis=0), 'dom', split_axis...  16.9 us
    all_to_all x1, starting transfers between devices, local(): lax.all_to_all(grid_rows, 'dom', split_axis=0, concat_axis=0, tiled=True)  13.2 us
    gather x1, local copies, waits for them, and re-layouts, local(): jnp.take(grid_table, enc_sender, axis=0)  9.17 us
  transfers between devices with their start and end apart: 5, of which 5 were waited for; matrix products, arithmetic and copies ran while one was open for 6% of the time, Pallas kernels for 0%

commit v1 on v0

v1 whole, which is shorter than its diff:
```python
import jax
import jax.numpy as jnp
from jax import lax
from jax.experimental import pallas as pl
from jax.experimental.pallas import tpu as pltpu
from jax.sharding import PartitionSpec as P

N_DOM = 32
SLOTS_GRID = 16
SLOTS_MESH = 8
BF = jnp.bfloat16
F32 = jnp.float32


def silu(v):
    half = 0.5 * v
    return half + half * jnp.tanh(half)


def dot(a, b):
    return jnp.dot(a, b, preferred_element_type=F32)


def lanes(shape):
    return lax.broadcasted_iota(jnp.int32, shape, 1).astype(F32)


def rows(shape):
    return lax.broadcasted_iota(jnp.int32, shape, 0).astype(F32)


def hot(index, offset):
    return jnp.where(index == lanes(index.shape) + offset, 1.0, 0.0).astype(BF)


def kernel(
    grid_in,
    w_embed,
    w_grid_send,
    enc_feat,
    w_enc_edge,
    enc_sender,
    enc_offset,
    lists,
    w_proc_send,
    w_proc_edge,
    w_proc_node,
    mesh_feat,
    mesh_sender,
    mesh_offset,
    w_skip,
    w_dec,
    w_dec_edge,
    dec_feat,
    dec_sender,
    dec_target,
    w_out,
    out,
    lists_got,
    grid_out,
    grid_got,
    mesh_out,
    mesh_got,
    lend_grid,
    lend_mesh,
    lend_dec,
    enc_rows,
    mesh_rows,
    dec_rows,
    enc_hot,
    mesh_hot,
    dec_hot,
    enc_to,
    mesh_to,
    dec_to,
    enc_count,
    mesh_count,
    dec_count,
    grid_latent,
    enc_table,
    enc_lent,
    mesh_table,
    enc_sum,
    enc_msg,
    mesh_msg,
    dec_msg,
    mesh_now,
    lists_sem,
    send_sem,
    recv_sem,
):
    me = lax.axis_index("dom")
    width = w_embed.shape[1]
    half = width // 2
    n_grid = grid_in.shape[0]
    n_mesh = mesh_to.shape[0]
    channels = grid_in.shape[1]

    def send_blocks(source, target, size, out_sem, in_sem):
        def step(r, carry):
            pltpu.make_async_remote_copy(
                src_ref=source(r),
                dst_ref=target.at[pl.ds((N_DOM - r) * size, size)],
                send_sem=out_sem,
                recv_sem=in_sem,
                device_id={"dom": lax.rem(me + r, N_DOM)},
                device_id_type=pl.DeviceIdType.MESH,
            ).start()
            return carry

        lax.fori_loop(1, N_DOM, step, 0)

    def wait_for(buffer, size, sem):
        part = buffer.at[pl.ds(size, (N_DOM - 1) * size)]
        pltpu.make_async_copy(part, part, sem).wait()

    barrier = pltpu.get_barrier_semaphore()

    def greet(r, carry):
        pl.semaphore_signal(
            barrier,
            inc=1,
            device_id={"dom": lax.rem(me + r, N_DOM)},
            device_id_type=pl.DeviceIdType.MESH,
        )
        return carry

    lax.fori_loop(1, N_DOM, greet, 0)

    lists_got[0:1] = jnp.zeros((1, 1, 128), jnp.int32)
    grid_got[0:16, :] = jnp.zeros((16, 256), BF)
    for k in range(3):
        mesh_got[k, 0:16, :] = jnp.zeros((16, 256), BF)

    pl.semaphore_wait(barrier, N_DOM - 1)
    send_blocks(
        lambda r: lists.at[pl.ds(lax.rem(me + r, N_DOM), 1)], lists_got, 1, lists_sem.at[0], lists_sem.at[1]
    )

    def embed(i, carry):
        part = pl.ds(pl.multiple_of(i * 256, 256), 256)
        latent = silu(dot(grid_in[part, :], w_embed[...])).astype(BF)
        grid_latent[part, :] = latent
        enc_table[part, :] = dot(latent, w_grid_send[...]).astype(BF)
        return carry

    lax.fori_loop(0, n_grid // 256, embed, 0)

    wait_for(lists_got, 1, lists_sem.at[1])
    listed = lists_got[:, 0, :].astype(F32)
    listed = jnp.transpose(jnp.concatenate([listed, jnp.zeros((96, 128), F32)], axis=0))
    for q in range(N_DOM):
        lend_grid[16 * q : 16 * q + 16, :] = jnp.broadcast_to(listed[0:16, q : q + 1], (16, 128))
        for lent, first in ((lend_mesh, 16), (lend_dec, 24)):
            column = jnp.broadcast_to(listed[first : first + 8, q : q + 1], (8, 128))
            lent[16 * q : 16 * q + 8, :] = column
            lent[16 * q + 8 : 16 * q + 16, :] = column + 128.0

    grid_out[...] = jnp.zeros_like(grid_out)
    for i in range(4):
        part = pl.ds(i * 128, 128)
        picks = jnp.concatenate(
            [hot(lend_grid[part, :], 128.0 * j) for j in range(n_grid // 128)], axis=1
        )
        grid_out[part, 0:channels] = dot(picks, grid_in[...]).astype(BF)
    send_blocks(
        lambda r: grid_out.at[pl.ds(pl.multiple_of(r * 16, 16), 16)],
        grid_got,
        16,
        send_sem.at[0],
        recv_sem.at[0],
    )

    def edge_rows(scratch, feat, sender, n_local, slots):
        edges = sender.shape[1]
        value = sender[...]
        lent = (value - n_local - me * slots) & (N_DOM * slots - 1)
        local = value < n_local
        scratch[...] = jnp.zeros_like(scratch)
        scratch[0:4, :] = feat[...].astype(F32)
        scratch[4:5, :] = jnp.where(local, value, -1).astype(F32)
        scratch[5:6, :] = jnp.where(local, -1, lent).astype(F32)

    def sender_hot(scratch, hots, n_local, n_lent):
        def step(i, carry):
            part = pl.ds(pl.multiple_of(i * 128, 128), 128)
            turned = jnp.transpose(
                jnp.concatenate([scratch[:, part], jnp.zeros((120, 128), F32)], axis=0)
            )
            local = jnp.broadcast_to(turned[:, 4:5], (128, 128))
            lent = jnp.broadcast_to(turned[:, 5:6], (128, 128))
            for j in range(n_local // 128):
                hots[part, 128 * j : 128 * j + 128] = hot(local, 128.0 * j)
            hots[part, n_local : n_local + 128] = turned.astype(BF)
            for j in range(n_lent // 128):
                at = n_local + 128 + 128 * j
                hots[part, at : at + 128] = hot(lent, 128.0 * j)
            return carry

        lax.fori_loop(0, hots.shape[0] // 128, step, 0)

    def receiver_hot(target, hots, count):
        n_rows = hots.shape[0]
        count[...] = jnp.zeros_like(count)

        def step(i, carry):
            part = pl.ds(pl.multiple_of(i * 128, 128), 128)
            wanted = jnp.broadcast_to(target[:, part].astype(F32), (n_rows, 128))
            same = jnp.where(wanted == rows((n_rows, 128)), 1.0, 0.0)
            hots[:, part] = same.astype(BF)
            count[...] += same
            return carry

        lax.fori_loop(0, hots.shape[1] // 128, step, 0)
        total = jnp.sum(count[...], axis=1, keepdims=True)
        count[...] = jnp.broadcast_to(jnp.maximum(total, 1.0), count.shape)

    def edge_weights(table, at, w_edge):
        table[at : at + 128, :] = jnp.zeros((128, width), BF)
        table[at : at + 4, :] = w_edge

    def mean(hots, messages, count):
        return dot(hots, messages) / jnp.concatenate([count] * (width // 128), axis=1)

    edge_rows(enc_rows, enc_feat, enc_sender, n_grid, SLOTS_GRID)
    sender_hot(enc_rows, enc_hot, n_grid, N_DOM * SLOTS_GRID)
    edge_weights(enc_table, n_grid, w_enc_edge[...])

    def enc_local(i, carry):
        part = pl.ds(pl.multiple_of(i * 512, 512), 512)
        enc_sum[part, :] = dot(enc_hot[part, 0 : n_grid + 128], enc_table[...])
        return carry

    lax.fori_loop(0, enc_sum.shape[0] // 512, enc_local, 0)
    receiver_hot(enc_offset, enc_to, enc_count)

    wait_for(grid_got, 16, recv_sem.at[0])

    def embed_lent(i, carry):
        part = pl.ds(pl.multiple_of(i * 256, 256), 256)
        latent = silu(dot(grid_got[part, 0:channels], w_embed[...])).astype(BF)
        enc_lent[part, :] = dot(latent, w_grid_send[...]).astype(BF)
        return carry

    lax.fori_loop(0, enc_lent.shape[0] // 256, embed_lent, 0)

    def enc_remote(i, carry):
        part = pl.ds(pl.multiple_of(i * 512, 512), 512)
        total = enc_sum[part, :] + dot(enc_hot[part, n_grid + 128 :], enc_lent[...])
        enc_msg[part, :] = silu(total).astype(BF)
        return carry

    lax.fori_loop(0, enc_sum.shape[0] // 512, enc_remote, 0)
    mesh_now[...] = mean(enc_to[...], enc_msg[...], enc_count[...]).astype(BF)

    def lend(k, lent, values):
        picks = jnp.concatenate([hot(lent[...], 0.0), hot(lent[...], 128.0)], axis=1)
        stacked = jnp.concatenate([values[:, 0:half], values[:, half:]], axis=0)
        mesh_out[k] = dot(picks, stacked).astype(BF)
        send_blocks(
            lambda r: mesh_out.at[k, pl.ds(pl.multiple_of(r * 16, 16), 16)],
            mesh_got.at[k],
            16,
            send_sem.at[k + 1],
            recv_sem.at[k + 1],
        )

    def borrow(k):
        wait_for(mesh_got.at[k], 16, recv_sem.at[k + 1])
        got = mesh_got[k].astype(F32).reshape(N_DOM, 16, half)
        low = got[:, 0:8, :].reshape(N_DOM * 8, half)
        high = got[:, 8:16, :].reshape(N_DOM * 8, half)
        mesh_table[256:512, :] = jnp.concatenate([low, high], axis=1).astype(BF)

    def messages_of(hots, messages):
        def step(i, carry):
            part = pl.ds(pl.multiple_of(i * 512, 512), 512)
            messages[part, :] = silu(dot(hots[part, :], mesh_table[...])).astype(BF)
            return carry

        lax.fori_loop(0, hots.shape[0] // 512, step, 0)

    for k in range(2):
        values = dot(mesh_now[...], w_proc_send[k]).astype(BF)
        lend(k, lend_mesh, values)
        mesh_table[0:128, :] = values
        edge_weights(mesh_table, 128, w_proc_edge[k])
        if k == 0:
            edge_rows(mesh_rows, mesh_feat, mesh_sender, n_mesh, SLOTS_MESH)
            sender_hot(mesh_rows, mesh_hot, n_mesh, N_DOM * SLOTS_MESH)
            receiver_hot(mesh_offset, mesh_to, mesh_count)
        else:
            edge_rows(dec_rows, dec_feat, dec_sender, n_mesh, SLOTS_MESH)
            sender_hot(dec_rows, dec_hot, n_mesh, N_DOM * SLOTS_MESH)
        borrow(k)
        messages_of(mesh_hot, mesh_msg)
        mesh_mean = mean(mesh_to[...], mesh_msg[...], mesh_count[...]).astype(BF)
        update = silu(dot(mesh_mean, w_proc_node[k]))
        mesh_now[...] = (mesh_now[...].astype(F32) + update).astype(BF)

    lend(2, lend_dec, mesh_now[...])
    mesh_table[0:128, :] = mesh_now[...]
    edge_weights(mesh_table, 128, w_dec_edge[...])
    receiver_hot(dec_target, dec_to, dec_count)
    borrow(2)
    messages_of(dec_hot, dec_msg)

    def decode(i, carry):
        part = pl.ds(pl.multiple_of(i * 256, 256), 256)
        grid_mean = mean(dec_to[part, :], dec_msg[...], dec_count[part, :]).astype(BF)
        mixed = dot(grid_mean, w_dec[...]) + dot(grid_latent[part, :], w_skip[...])
        out[part, :] = dot(silu(mixed).astype(BF), w_out[...]).astype(BF)
        return carry

    lax.fori_loop(0, n_grid // 256, decode, 0)

    wait_for(lists_got, 1, lists_sem.at[0])
    wait_for(grid_out, 16, send_sem.at[0])
    for k in range(3):
        wait_for(mesh_out.at[k], 16, send_sem.at[k + 1])


def local(
    grid_in,
    w_embed,
    w_grid_send,
    enc_feat,
    w_enc_edge,
    enc_sender,
    enc_offset,
    grid_rows,
    w_proc_send,
    w_proc_edge,
    w_proc_node,
    mesh_feat,
    mesh_sender,
    mesh_offset,
    mesh_rows,
    w_skip,
    w_dec,
    w_dec_edge,
    dec_feat,
    dec_sender,
    dec_offset,
    dec_block,
    dec_rows,
    w_out,
):
    n_grid = grid_in.shape[0]
    width = w_embed.shape[1]
    n_mesh = 128
    enc, mesh, dec = enc_sender.shape[0], mesh_sender.shape[0], dec_sender.shape[0]
    lists = jnp.concatenate(
        [grid_rows, mesh_rows, dec_rows, jnp.zeros((N_DOM, 96), jnp.int32)], axis=1
    ).reshape(N_DOM, 1, 128)
    dec_target = jnp.where(
        dec_offset >= 0, jnp.repeat(dec_block * 128, 128) + dec_offset, -1
    )
    operands = (
        grid_in,
        w_embed,
        w_grid_send,
        enc_feat,
        w_enc_edge,
        enc_sender.reshape(1, enc),
        enc_offset.reshape(1, enc),
        lists,
        w_proc_send,
        w_proc_edge,
        w_proc_node,
        mesh_feat,
        mesh_sender.reshape(1, mesh),
        mesh_offset.reshape(1, mesh),
        w_skip,
        w_dec,
        w_dec_edge,
        dec_feat,
        dec_sender.reshape(1, dec),
        dec_target.reshape(1, dec),
        w_out,
    )
    whole = pl.BlockSpec(memory_space=pltpu.VMEM)
    return pl.pallas_call(
        kernel,
        out_shape=jax.ShapeDtypeStruct((n_grid, w_out.shape[1]), BF),
        in_specs=[whole] * len(operands),
        out_specs=whole,
        scratch_shapes=[
            pltpu.VMEM((N_DOM, 1, 128), jnp.int32),
            pltpu.VMEM((512, 256), BF),
            pltpu.VMEM((512, 256), BF),
            pltpu.VMEM((3, 512, 256), BF),
            pltpu.VMEM((3, 512, 256), BF),
            pltpu.VMEM((512, 128), F32),
            pltpu.VMEM((512, 128), F32),
            pltpu.VMEM((512, 128), F32),
            pltpu.VMEM((8, enc), F32),
            pltpu.VMEM((8, mesh), F32),
            pltpu.VMEM((8, dec), F32),
            pltpu.VMEM((enc, n_grid + 128 + 512), BF),
            pltpu.VMEM((mesh, 512), BF),
            pltpu.VMEM((dec, 512), BF),
            pltpu.VMEM((n_mesh, enc), BF),
            pltpu.VMEM((n_mesh, mesh), BF),
            pltpu.VMEM((n_grid, dec), BF),
            pltpu.VMEM((n_mesh, 128), F32),
            pltpu.VMEM((n_mesh, 128), F32),
            pltpu.VMEM((n_grid, 128), F32),
            pltpu.VMEM((n_grid, width), BF),
            pltpu.VMEM((n_grid + 128, width), BF),
            pltpu.VMEM((512, width), BF),
            pltpu.VMEM((512, width), BF),
            pltpu.VMEM((enc, width), F32),
            pltpu.VMEM((enc, width), BF),
            pltpu.VMEM((mesh, width), BF),
            pltpu.VMEM((dec, width), BF),
            pltpu.VMEM((n_mesh, width), BF),
            pltpu.SemaphoreType.DMA((2,)),
            pltpu.SemaphoreType.DMA((4,)),
            pltpu.SemaphoreType.DMA((4,)),
        ],
        compiler_params=pltpu.CompilerParams(
            collective_id=0, has_side_effects=True, vmem_limit_bytes=56 * 1024 * 1024
        ),
        name="graph_weather",
    )(*operands)


def solution(mesh):
    in_specs = (
        P(("member", "dom"), None),
        P(),
        P(),
        P(None, "dom"),
        P(),
        P("dom"),
        P("dom"),
        P("dom", None),
        P(),
        P(),
        P(),
        P(None, "dom"),
        P("dom"),
        P("dom"),
        P("dom", None),
        P(),
        P(),
        P(),
        P(None, "dom"),
        P("dom"),
        P("dom"),
        P("dom"),
        P("dom", None),
        P(),
    )
    out_specs = P(("member", "dom"), None)
    return jax.shard_map(local, mesh=mesh, in_specs=in_specs, out_specs=out_specs, check_vma=False)
```

time: 383 us -> 81 us (0.21)
  waiting for transfers between devices: 258 us -> 0 us
  Pallas kernels: 0 us -> 71.5 us
  local copies, waits for them, and re-layouts: 63.3 us -> 7.16 us
  matrix products: 27.5 us -> 0 us
  starting transfers between devices: 17.4 us -> 0 us
  between operations: 13.6 us -> 0.02 us
    all_gather x3 -> x0, waiting for transfers between devices: 235 us -> none  [spread(): whole_mesh = lax.all_gather(values, 'dom', axis=0, tiled=True)]
    pallas_call x0 -> x1, Pallas kernels: none -> 71.5 us  [local(): pl.pallas_call(kernel, out_shape=jax.ShapeDtypeStruct((n_grid, w_out.shap...]
    gather x7 -> x0, local copies, waits for them, and re-layouts: 58.5 us -> none  [the longest x3 29.5 us: spread(): return jnp.take(whole_mesh, index, axis=0)]
    dot_general x15 -> x0, matrix products: 27.5 us -> none  [the longest x3 5.87 us: mean_local(): jnp.dot(onehot.astype(jnp.bfloat16), messages, preferred_element_type=jnp...]
    all_to_all x2 -> x0, waiting for transfers between devices: 22.9 us -> none  [the longest x1 16.9 us: local(): lax.all_to_all(jnp.take(grid_send, grid_lists, axis=0), 'dom', split_axis...]
    all_to_all x2 -> x0, starting transfers between devices: 17.1 us -> none  [the longest x1 13.2 us: local(): lax.all_to_all(grid_rows, 'dom', split_axis=0, concat_axis=0, tiled=True)]
  transfers between devices with their start and end apart: 5 -> 0, of which waited for: 5 -> 0; matrix products, arithmetic and copies ran while one was open for 6% -> 0% of each run, Pallas kernels for 0% -> 0%
where the time goes in v1:
time: 81 us; the launch traced here: 80.7 us
  Pallas kernels  71.5 us (88%)
  local copies, waits for them, and re-layouts  7.16 us (9%)
  other arithmetic  2.06 us (3%)
    pallas_call x1, Pallas kernels, local(): pl.pallas_call(kernel, out_shape=jax.ShapeDtypeStruct((n_grid, w_out.shap...  71.5 us
    unnamed x9, local copies, waits for them, and re-layouts  5.07 us
    pallas_call x1, local copies, waits for them, and re-layouts, local(): pl.pallas_call(kernel, out_shape=jax.ShapeDtypeStruct((n_grid, w_out.shap...  2.02 us

profile of v1, /device:TPU:56, one launch (start us, length us, event | category | flops | bytes accessed | tf_op | source)
XLA Modules:
  0.0 80.7 jit_solution(9569938785351939656)
XLA Ops:
  0.0 0.0 copy-start.1
  0.0 0.0 copy-start
  0.0 0.7 broadcast_multiply_fusion
  0.7 0.1 pad.3.clone
  0.8 0.0 copy-done.1
  0.8 0.7 fusion
  1.5 0.8 copy.25
  2.2 0.8 copy.26
  3.0 0.8 copy.27
  3.8 0.7 add_add_fusion
  4.4 1.8 %copy.29.w_out = bf16[512,227]{1,0:T(8,128)(2,1)} copy(bf16[512,227]{0,1:T(8,128)(2,1)} %param.47) | data formatting | bytes 464896 | tf_op args[23]
  6.2 0.0 copy-done
  6.2 1.0 %copy.28.grid_in = bf16[1024,227]{1,0:T(8,128)(2,1)} copy(bf16[1024,227]{0,1:T(8,128)(2,1)S(1)} %copy-done) | data formatting | bytes 929792 | tf_op args[0]
  7.2 71.5 %graph_weather.1 = bf16[1024,227]{1,0:T(8,128)(2,1)} custom-call(bf16[1024,227]{1,0:T(8,128)(2,1)} %copy.28.grid_in, bf16[227,512]{1,0:T(8,128)(2,1)} %w_embed.1, bf16[512,512]{1,0:T(8,128)(2,1)} %w_grid_send.1, bf16[4,2048]{1,0:T(4,128)(2,1)} %enc_feat.1, bf16[4,512]{1,0:T(4,128)(2,1)} %w_enc_edge.1, s32[1,2048]{1,0:T(1,128)} %bitcast.14, ...), custom_call_target="tpu_custom_call" | custom-call | tf_op jit(solution)/shard_map/graph_weather/pallas_call | solution.py:383
  78.7 2.0 %copy.30 = bf16[1024,227]{0,1:T(8,128)(2,1)} copy(bf16[1024,227]{1,0:T(8,128)(2,1)} %graph_weather.1) | data formatting | bytes 929792 | tf_op jit(solution)/shard_map/graph_weather/pallas_call | solution.py:383
  (1 shorter events, 0.0 us)
Async XLA Ops:
  0.0 0.8 copy-start.1
  0.0 6.2 %copy-start = (bf16[1024,227]{0,1:T(8,128)(2,1)S(1)}, bf16[1024,227]{0,1:T(8,128)(2,1)}, u32[]{:S(2)}) copy-start(bf16[1024,227]{0,1:T(8,128)(2,1)} %param.24) | copy-start | bytes 1394692

commit v2 on v1

--- a/solution.py
+++ b/solution.py
@@ -19,6 +19,10 @@
 
 def dot(a, b):
     return jnp.dot(a, b, preferred_element_type=F32)
+
+
+def dot_turned(a, b):
+    return lax.dot_general(a, b, (((1,), (1,)), ((), ())), preferred_element_type=F32)
 
 
 def lanes(shape):
@@ -41,7 +45,9 @@
     w_enc_edge,
     enc_sender,
     enc_offset,
-    lists,
+    grid_list,
+    mesh_list,
+    dec_list,
     w_proc_send,
     w_proc_edge,
     w_proc_node,
@@ -53,9 +59,11 @@
     w_dec_edge,
     dec_feat,
     dec_sender,
-    dec_target,
+    dec_offset,
+    dec_block,
     w_out,
     out,
+    lists_out,
     lists_got,
     grid_out,
     grid_got,
@@ -85,6 +93,16 @@
     mesh_msg,
     dec_msg,
     mesh_now,
+    grid_turned,
+    grid_held,
+    w_embed_held,
+    w_grid_send_held,
+    w_proc_send_held,
+    w_proc_node_held,
+    w_skip_held,
+    w_dec_held,
+    w_out_held,
+    load_sem,
     lists_sem,
     send_sem,
     recv_sem,
@@ -92,9 +110,8 @@
     me = lax.axis_index("dom")
     width = w_embed.shape[1]
     half = width // 2
-    n_grid = grid_in.shape[0]
+    channels, n_grid = grid_in.shape
     n_mesh = mesh_to.shape[0]
-    channels = grid_in.shape[1]
 
     def send_blocks(source, target, size, out_sem, in_sem):
         def step(r, carry):
@@ -127,6 +144,30 @@
 
     lax.fori_loop(1, N_DOM, greet, 0)
 
+    loads = [
+        pltpu.make_async_copy(held_from, held, load_sem.at[i])
+        for i, (held_from, held) in enumerate(
+            (
+                (grid_in, grid_held),
+                (w_embed, w_embed_held),
+                (w_grid_send, w_grid_send_held),
+                (w_proc_send, w_proc_send_held),
+                (w_proc_node, w_proc_node_held),
+                (w_skip, w_skip_held),
+                (w_dec, w_dec_held),
+                (w_out, w_out_held),
+            )
+        )
+    ]
+    for load in loads:
+        load.start()
+
+    slots = jnp.concatenate([grid_list[...], mesh_list[...], dec_list[...]], axis=0).astype(F32)
+    slots = jnp.concatenate([slots, jnp.zeros((N_DOM, 96), F32)], axis=1)
+    slots = jnp.transpose(jnp.concatenate([slots, jnp.zeros((96, 128), F32)], axis=0))
+    for p in range(N_DOM):
+        lists_out[p] = slots[p : p + 1, :].astype(jnp.int32)
+
     lists_got[0:1] = jnp.zeros((1, 1, 128), jnp.int32)
     grid_got[0:16, :] = jnp.zeros((16, 256), BF)
     for k in range(3):
@@ -134,14 +175,19 @@
 
     pl.semaphore_wait(barrier, N_DOM - 1)
     send_blocks(
-        lambda r: lists.at[pl.ds(lax.rem(me + r, N_DOM), 1)], lists_got, 1, lists_sem.at[0], lists_sem.at[1]
+        lambda r: lists_out.at[pl.ds(lax.rem(me + r, N_DOM), 1)], lists_got, 1, lists_sem.at[0], lists_sem.at[1]
     )
+
+    loads[0].wait()
+    loads[1].wait()
+    loads[2].wait()
 
     def embed(i, carry):
         part = pl.ds(pl.multiple_of(i * 256, 256), 256)
-        latent = silu(dot(grid_in[part, :], w_embed[...])).astype(BF)
+        grid_turned[...] = jnp.transpose(grid_held[:, part])
+        latent = silu(dot(grid_turned[...], w_embed_held[...])).astype(BF)
         grid_latent[part, :] = latent
-        enc_table[part, :] = dot(latent, w_grid_send[...]).astype(BF)
+        enc_table[part, :] = dot(latent, w_grid_send_held[...]).astype(BF)
         return carry
 
     lax.fori_loop(0, n_grid // 256, embed, 0)
@@ -162,7 +208,7 @@
         picks = jnp.concatenate(
             [hot(lend_grid[part, :], 128.0 * j) for j in range(n_grid // 128)], axis=1
         )
-        grid_out[part, 0:channels] = dot(picks, grid_in[...]).astype(BF)
+        grid_out[part, 0:channels] = dot_turned(picks, grid_held[...]).astype(BF)
     send_blocks(
         lambda r: grid_out.at[pl.ds(pl.multiple_of(r * 16, 16), 16)],
         grid_got,
@@ -199,13 +245,16 @@
 
         lax.fori_loop(0, hots.shape[0] // 128, step, 0)
 
-    def receiver_hot(target, hots, count):
+    def receiver_hot(target, hots, count, block=None):
         n_rows = hots.shape[0]
         count[...] = jnp.zeros_like(count)
 
         def step(i, carry):
             part = pl.ds(pl.multiple_of(i * 128, 128), 128)
-            wanted = jnp.broadcast_to(target[:, part].astype(F32), (n_rows, 128))
+            wanted = target[:, part]
+            if block is not None:
+                wanted = jnp.where(wanted >= 0, wanted + 128 * block[0, i], -1)
+            wanted = jnp.broadcast_to(wanted.astype(F32), (n_rows, 128))
             same = jnp.where(wanted == rows((n_rows, 128)), 1.0, 0.0)
             hots[:, part] = same.astype(BF)
             count[...] += same
@@ -238,8 +287,8 @@
 
     def embed_lent(i, carry):
         part = pl.ds(pl.multiple_of(i * 256, 256), 256)
-        latent = silu(dot(grid_got[part, 0:channels], w_embed[...])).astype(BF)
-        enc_lent[part, :] = dot(latent, w_grid_send[...]).astype(BF)
+        latent = silu(dot(grid_got[part, 0:channels], w_embed_held[...])).astype(BF)
+        enc_lent[part, :] = dot(latent, w_grid_send_held[...]).astype(BF)
         return carry
 
     lax.fori_loop(0, enc_lent.shape[0] // 256, embed_lent, 0)
@@ -280,8 +329,10 @@
 
         lax.fori_loop(0, hots.shape[0] // 512, step, 0)
 
+    for load in loads[3:]:
+        load.wait()
     for k in range(2):
-        values = dot(mesh_now[...], w_proc_send[k]).astype(BF)
+        values = dot(mesh_now[...], w_proc_send_held[k]).astype(BF)
         lend(k, lend_mesh, values)
         mesh_table[0:128, :] = values
         edge_weights(mesh_table, 128, w_proc_edge[k])
@@ -295,21 +346,21 @@
         borrow(k)
         messages_of(mesh_hot, mesh_msg)
         mesh_mean = mean(mesh_to[...], mesh_msg[...], mesh_count[...]).astype(BF)
-        update = silu(dot(mesh_mean, w_proc_node[k]))
+        update = silu(dot(mesh_mean, w_proc_node_held[k]))
         mesh_now[...] = (mesh_now[...].astype(F32) + update).astype(BF)
 
     lend(2, lend_dec, mesh_now[...])
     mesh_table[0:128, :] = mesh_now[...]
     edge_weights(mesh_table, 128, w_dec_edge[...])
-    receiver_hot(dec_target, dec_to, dec_count)
+    receiver_hot(dec_offset, dec_to, dec_count, dec_block)
     borrow(2)
     messages_of(dec_hot, dec_msg)
 
     def decode(i, carry):
         part = pl.ds(pl.multiple_of(i * 256, 256), 256)
         grid_mean = mean(dec_to[part, :], dec_msg[...], dec_count[part, :]).astype(BF)
-        mixed = dot(grid_mean, w_dec[...]) + dot(grid_latent[part, :], w_skip[...])
-        out[part, :] = dot(silu(mixed).astype(BF), w_out[...]).astype(BF)
+        mixed = dot(grid_mean, w_dec_held[...]) + dot(grid_latent[part, :], w_skip_held[...])
+        out[:, part] = dot_turned(w_out_held[...], silu(mixed).astype(BF)).astype(BF)
         return carry
 
     lax.fori_loop(0, n_grid // 256, decode, 0)
@@ -350,21 +401,17 @@
     width = w_embed.shape[1]
     n_mesh = 128
     enc, mesh, dec = enc_sender.shape[0], mesh_sender.shape[0], dec_sender.shape[0]
-    lists = jnp.concatenate(
-        [grid_rows, mesh_rows, dec_rows, jnp.zeros((N_DOM, 96), jnp.int32)], axis=1
-    ).reshape(N_DOM, 1, 128)
-    dec_target = jnp.where(
-        dec_offset >= 0, jnp.repeat(dec_block * 128, 128) + dec_offset, -1
-    )
     operands = (
-        grid_in,
+        grid_in.T,
         w_embed,
         w_grid_send,
         enc_feat,
         w_enc_edge,
         enc_sender.reshape(1, enc),
         enc_offset.reshape(1, enc),
-        lists,
+        grid_rows.T,
+        mesh_rows.T,
+        dec_rows.T,
         w_proc_send,
         w_proc_edge,
         w_proc_node,
@@ -376,16 +423,23 @@
         w_dec_edge,
         dec_feat,
         dec_sender.reshape(1, dec),
-        dec_target.reshape(1, dec),
-        w_out,
+        dec_offset.reshape(1, dec),
+        dec_block.reshape(1, dec_block.shape[0]),
+        w_out.T,
     )
     whole = pl.BlockSpec(memory_space=pltpu.VMEM)
-    return pl.pallas_call(
+    far = pl.BlockSpec(memory_space=pl.ANY)
+    in_specs = [whole] * len(operands)
+    for i in (0, 1, 2, 10, 12, 16, 17, 23):
+        in_specs[i] = far
+    in_specs[22] = pl.BlockSpec(memory_space=pltpu.SMEM)
+    forecast = pl.pallas_call(
         kernel,
-        out_shape=jax.ShapeDtypeStruct((n_grid, w_out.shape[1]), BF),
-        in_specs=[whole] * len(operands),
+        out_shape=jax.ShapeDtypeStruct((w_out.shape[1], n_grid), BF),
+        in_specs=in_specs,
         out_specs=whole,
         scratch_shapes=[
+            pltpu.VMEM((N_DOM, 1, 128), jnp.int32),
             pltpu.VMEM((N_DOM, 1, 128), jnp.int32),
             pltpu.VMEM((512, 256), BF),
             pltpu.VMEM((512, 256), BF),
@@ -415,6 +469,16 @@
             pltpu.VMEM((mesh, width), BF),
             pltpu.VMEM((dec, width), BF),
             pltpu.VMEM((n_mesh, width), BF),
+            pltpu.VMEM((256, grid_in.shape[1]), BF),
+            pltpu.VMEM(grid_in.shape[::-1], BF),
+            pltpu.VMEM(w_embed.shape, BF),
+            pltpu.VMEM(w_grid_send.shape, BF),
+            pltpu.VMEM(w_proc_send.shape, BF),
+            pltpu.VMEM(w_proc_node.shape, BF),
+            pltpu.VMEM(w_skip.shape, BF),
+            pltpu.VMEM(w_dec.shape, BF),
+            pltpu.VMEM(w_out.shape[::-1], BF),
+            pltpu.SemaphoreType.DMA((8,)),
             pltpu.SemaphoreType.DMA((2,)),
             pltpu.SemaphoreType.DMA((4,)),
             pltpu.SemaphoreType.DMA((4,)),
@@ -424,6 +488,7 @@
         ),
         name="graph_weather",
     )(*operands)
+    return forecast.T
 
 
 def solution(mesh):

time: 81 us -> 72.7 us (0.90)
  local copies, waits for them, and re-layouts: 7.16 us -> 1.83 us
  other arithmetic: 2.06 us -> 0 us
  Pallas kernels: 71.5 us -> 70.6 us
    unnamed x9 -> x1, local copies, waits for them, and re-layouts: 5.07 us -> 1.83 us
    pallas_call x1 -> x0, local copies, waits for them, and re-layouts: 2.02 us -> none  [local(): pl.pallas_call(kernel, out_shape=jax.ShapeDtypeStruct((n_grid, w_out.shap...]
    pallas_call x1, Pallas kernels: 71.5 us -> 70.6 us  [local(): pl.pallas_call(kernel, out_shape=jax.ShapeDtypeStruct((w_out.shape[1], n_...]
where the time goes in v2:
time: 72.7 us; the launch traced here: 72.4 us
  Pallas kernels  70.6 us (97%)
  local copies, waits for them, and re-layouts  1.83 us (3%)
    pallas_call x1, Pallas kernels, local(): pl.pallas_call(kernel, out_shape=jax.ShapeDtypeStruct((w_out.shape[1], n_...  70.6 us
    unnamed x1, local copies, waits for them, and re-layouts  1.83 us

profile of v2, /device:TPU:56, one launch (start us, length us, event | category | flops | bytes accessed | tf_op | source)
XLA Modules:
  0.0 72.4 jit_solution(12751415833304533906)
XLA Ops:
  0.0 70.6 %graph_weather.1 = bf16[227,1024]{1,0:T(8,128)(2,1)} custom-call(bf16[227,1024]{1,0:T(8,128)(2,1)} %bitcast.14, bf16[227,512]{1,0:T(8,128)(2,1)} %w_embed.1, bf16[512,512]{1,0:T(8,128)(2,1)} %w_grid_send.1, bf16[4,2048]{1,0:T(4,128)(2,1)} %enc_feat.1, bf16[4,512]{1,0:T(4,128)(2,1)} %w_enc_edge.1, s32[1,2048]{1,0:T(1,128)} %bitcast.18, s32[1,2048]{1,0:T(1,128)} %bitcast.19, ...), custom_call_target="tpu_custom_call" | custom-call | tf_op jit(solution)/shard_map/graph_weather/pallas_call | solution.py:436
  70.6 1.8 %copy.26 = bf16[1024,227]{0,1:T(8,128)(2,1)} copy(bf16[1024,227]{0,1:T(8,128)(2,1)} %bitcast.13) | data formatting | bytes 929792

commit v3 on v2

v3 whole, which is shorter than its diff:
```python
import jax
import jax.numpy as jnp
from jax import lax
from jax.experimental import pallas as pl
from jax.experimental.pallas import tpu as pltpu
from jax.sharding import PartitionSpec as P

N_Z, N_X = 8, 4
N_DOM = N_Z * N_X
SLOTS_GRID = 16
SLOTS_MESH = 8
BF = jnp.bfloat16
F32 = jnp.float32


def silu_of_half(half):
    return half + half * jnp.tanh(half)


def silu(v):
    return silu_of_half(0.5 * v)


def dot(a, b):
    return jnp.dot(a, b, preferred_element_type=F32)


def dot_turned(a, b):
    return lax.dot_general(a, b, (((1,), (1,)), ((), ())), preferred_element_type=F32)


def lanes(shape):
    return lax.broadcasted_iota(jnp.int32, shape, 1).astype(F32)


def rows(shape):
    return lax.broadcasted_iota(jnp.int32, shape, 0).astype(F32)


def hot(index, offset, value=1.0):
    return jnp.where(index == lanes(index.shape) + offset, value, 0.0).astype(BF)


def hops(offset):
    dz, dx = offset
    return min(dz, N_Z - dz) + min(dx, N_X - dx)


OFFSETS = [(dz, dx) for dz in range(N_Z) for dx in range(N_X) if (dz, dx) != (0, 0)]
FAR_FIRST = sorted(OFFSETS, key=lambda offset: -hops(offset))


def plain_slot(dz, dx):
    return (dz % N_Z) * N_X + dx % N_X


def far_slot(dz, dx):
    dz = dz % N_Z
    return (dz + 4 if dz < 3 else dz - 3 if dz < 7 else 7) * N_X + dx % N_X


def kernel(
    grid_in,
    w_embed,
    w_grid_send,
    enc_feat,
    w_enc_edge,
    enc_sender,
    enc_offset,
    grid_list,
    mesh_list,
    dec_list,
    w_proc_send,
    w_proc_edge,
    w_proc_node,
    mesh_feat,
    mesh_sender,
    mesh_offset,
    w_skip,
    w_dec,
    w_dec_edge,
    dec_feat,
    dec_sender,
    dec_offset,
    dec_block,
    w_out,
    out,
    lists_out,
    lists_got,
    grid_out,
    grid_got,
    mesh_out,
    mesh_got,
    lend_grid,
    lend_mesh,
    lend_dec,
    lend_hot,
    enc_rows,
    mesh_rows,
    dec_rows,
    enc_hot,
    mesh_hot,
    dec_hot,
    enc_to,
    mesh_to,
    dec_to,
    enc_count,
    mesh_count,
    dec_count,
    grid_latent,
    enc_table,
    enc_lent,
    mesh_table,
    edge_sum,
    edge_msg,
    mesh_now,
    mesh_mean,
    mixed,
    grid_turned,
    grid_held,
    w_embed_held,
    w_grid_send_held,
    w_proc_send_held,
    w_proc_node_held,
    w_skip_held,
    w_dec_held,
    w_out_held,
    load_sem,
    lists_sem,
    send_sem,
    recv_sem,
):
    me = lax.axis_index("dom")
    me_z, me_x = me // N_X, lax.rem(me, N_X)
    width = w_embed.shape[1]
    half = width // 2
    quarter = width // 4
    channels, n_grid = grid_in.shape
    n_mesh = mesh_to.shape[0]
    near = n_grid + 128

    def peer(dz, dx):
        return lax.rem(me_z + dz, N_Z) * N_X + lax.rem(me_x + dx, N_X)

    def send(source, target, out_sem, in_sem, offset):
        pltpu.make_async_remote_copy(
            src_ref=source,
            dst_ref=target,
            send_sem=out_sem,
            recv_sem=in_sem,
            device_id={"dom": peer(*offset)},
            device_id_type=pl.DeviceIdType.MESH,
        ).start()

    def wait_for(part, sem):
        pltpu.make_async_copy(part, part, sem).wait()

    barrier = pltpu.get_barrier_semaphore()
    for offset in FAR_FIRST:
        pl.semaphore_signal(
            barrier,
            inc=1,
            device_id={"dom": peer(*offset)},
            device_id_type=pl.DeviceIdType.MESH,
        )

    loads = [
        pltpu.make_async_copy(held_from, held, load_sem.at[i])
        for i, (held_from, held) in enumerate(
            (
                (grid_in, grid_held),
                (w_embed, w_embed_held),
                (w_grid_send, w_grid_send_held),
                (w_proc_send, w_proc_send_held),
                (w_proc_node, w_proc_node_held),
                (w_skip, w_skip_held),
                (w_dec, w_dec_held),
                (w_out, w_out_held),
            )
        )
    ]
    for load in loads:
        load.start()

    slots = jnp.concatenate([grid_list[...], mesh_list[...], dec_list[...]], axis=0).astype(F32)
    slots = jnp.concatenate([slots, jnp.zeros((N_DOM, 96), F32)], axis=1)
    slots = jnp.transpose(jnp.concatenate([slots, jnp.zeros((96, 128), F32)], axis=0))
    for p in range(N_DOM):
        lists_out[p] = slots[p : p + 1, :].astype(jnp.int32)

    lists_got[0:1] = jnp.zeros((1, 1, 128), jnp.int32)
    own = 16 * far_slot(0, 0)
    grid_got[own : own + 16, :] = jnp.zeros((16, 256), BF)
    for k in range(3):
        for h in range(2):
            mesh_got[k, h, 0:16, :] = jnp.zeros((16, quarter), BF)

    for load in loads[0:3]:
        load.wait()

    def embed(i, carry):
        part = pl.ds(pl.multiple_of(i * 256, 256), 256)
        grid_turned[...] = jnp.transpose(grid_held[:, part])
        latent = silu(dot(grid_turned[...], w_embed_held[...])).astype(BF)
        grid_latent[part, :] = latent
        enc_table[part, :] = dot(latent, w_grid_send_held[...]).astype(BF)
        return carry

    lax.fori_loop(0, n_grid // 256, embed, 0)

    pl.semaphore_wait(barrier, N_DOM - 1)
    for dz, dx in FAR_FIRST:
        send(
            lists_out.at[pl.ds(peer(dz, dx), 1)],
            lists_got.at[pl.ds(plain_slot(-dz, -dx), 1)],
            lists_sem.at[0],
            lists_sem.at[1],
            (dz, dx),
        )

    def edge_rows(scratch, feat, sender, n_local, n_slots, first):
        value = sender[...]
        shifted = jnp.maximum(value - n_local, 0)
        log_slots = n_slots.bit_length() - 1
        giver = shifted >> log_slots
        dz = ((giver >> 2) - me_z) & (N_Z - 1)
        dx = ((giver & (N_X - 1)) - me_x) & (N_X - 1)
        if first:
            dz = jnp.where(dz < 3, dz + 4, jnp.where(dz < 7, dz - 3, 7))
        lent = ((dz * N_X + dx) << log_slots) + (shifted & (n_slots - 1))
        local = value < n_local
        scratch[...] = jnp.zeros_like(scratch)
        scratch[0:4, :] = 0.5 * feat[...].astype(F32)
        scratch[4:5, :] = jnp.where(local, value, -1).astype(F32)
        scratch[5:6, :] = jnp.where(local, -1, lent).astype(F32)

    def sender_hot(scratch, hots, n_local, n_lent):
        def step(i, carry):
            part = pl.ds(pl.multiple_of(i * 128, 128), 128)
            turned = jnp.transpose(
                jnp.concatenate([scratch[:, part], jnp.zeros((120, 128), F32)], axis=0)
            )
            local = jnp.broadcast_to(turned[:, 4:5], (128, 128))
            lent = jnp.broadcast_to(turned[:, 5:6], (128, 128))
            for j in range(n_local // 128):
                hots[part, 128 * j : 128 * j + 128] = hot(local, 128.0 * j, 0.5)
            hots[part, n_local : n_local + 128] = turned.astype(BF)
            for j in range(n_lent // 128):
                at = n_local + 128 + 128 * j
                hots[part, at : at + 128] = hot(lent, 128.0 * j, 0.5)
            return carry

        lax.fori_loop(0, hots.shape[0] // 128, step, 0, unroll=4)

    def receiver_hot(target, hots, count, block=None):
        n_rows = hots.shape[0]
        count[...] = jnp.zeros_like(count)

        def step(i, carry):
            part = pl.ds(pl.multiple_of(i * 128, 128), 128)
            wanted = target[:, part]
            if block is not None:
                wanted = jnp.where(wanted >= 0, wanted + 128 * block[0, i], -1)
            wanted = jnp.broadcast_to(wanted.astype(F32), (n_rows, 128))
            same = jnp.where(wanted == rows((n_rows, 128)), 1.0, 0.0)
            hots[:, part] = same.astype(BF)
            count[...] += same
            return carry

        lax.fori_loop(0, hots.shape[1] // 128, step, 0, unroll=2)
        total = jnp.sum(count[...], axis=1, keepdims=True)
        count[...] = jnp.broadcast_to(jnp.maximum(total, 1.0), count.shape)

    def edge_weights(table, at, w_edge):
        table[at : at + 128, :] = jnp.zeros((128, width), BF)
        table[at : at + 4, :] = w_edge

    def mean(hots, messages, count):
        columns = messages.shape[1]
        return dot(hots, messages) / jnp.concatenate([count] * (columns // 128), axis=1)

    edge_rows(enc_rows, enc_feat, enc_sender, n_grid, SLOTS_GRID, True)
    sender_hot(enc_rows, enc_hot, n_grid, N_DOM * SLOTS_GRID)
    receiver_hot(enc_offset, enc_to, enc_count)
    edge_weights(enc_table, n_grid, w_enc_edge[...])

    wait_for(lists_got.at[pl.ds(1, N_DOM - 1)], lists_sem.at[1])
    listed = lists_got[:, 0, :].astype(F32)
    listed = jnp.transpose(jnp.concatenate([listed, jnp.zeros((96, 128), F32)], axis=0))
    for q in range(N_DOM):
        lend_grid[16 * q : 16 * q + 16, :] = jnp.broadcast_to(listed[0:16, q : q + 1], (16, 128))
        for lent, first in ((lend_mesh, 16), (lend_dec, 24)):
            column = jnp.broadcast_to(listed[first : first + 8, q : q + 1], (8, 128))
            lent[16 * q : 16 * q + 8, :] = column
            lent[16 * q + 8 : 16 * q + 16, :] = column + 128.0

    for group, pair in ((0, (4, 5)), (0, (3, 2)), (1, (6, 7)), (1, (1, 0))):
        part = pl.ds(64 * min(pair), 128)
        picks = jnp.concatenate(
            [hot(lend_grid[part, :], 128.0 * j) for j in range(n_grid // 128)], axis=1
        )
        grid_out[part, channels - channels % 128 :] = jnp.zeros((128, 128), BF)
        grid_out[part, 0:channels] = dot_turned(picks, grid_held[...]).astype(BF)
        for dz in pair:
            for dx in (2, 1, 3, 0):
                if (dz, dx) != (0, 0):
                    send(
                        grid_out.at[pl.ds(16 * plain_slot(dz, dx), 16)],
                        grid_got.at[pl.ds(16 * far_slot(-dz, -dx), 16)],
                        send_sem.at[group],
                        recv_sem.at[group],
                        (dz, dx),
                    )

    def local_sums(hots, columns, table):
        def step(i, carry):
            part = pl.ds(pl.multiple_of(i * 512, 512), 512)
            edge_sum[part, :] = dot(hots[part, 0:columns], table)
            return carry

        lax.fori_loop(0, hots.shape[0] // 512, step, 0)

    local_sums(enc_hot, near, enc_table[...])
    edge_rows(mesh_rows, mesh_feat, mesh_sender, n_mesh, SLOTS_MESH, False)
    sender_hot(mesh_rows, mesh_hot, n_mesh, N_DOM * SLOTS_MESH)
    receiver_hot(mesh_offset, mesh_to, mesh_count)
    for k, lent in enumerate((lend_mesh, lend_dec)):
        lend_hot[k] = jnp.concatenate([hot(lent[...], 0.0), hot(lent[...], 128.0)], axis=1)

    def embed_lent(group):
        wait_for(
            grid_got.at[pl.ds(256 * group + 16 * group, 256 - 16 * group)], recv_sem.at[group]
        )
        part = pl.ds(256 * group, 256)
        latent = silu(dot(grid_got[part, 0:channels], w_embed_held[...])).astype(BF)
        enc_lent[...] = dot(latent, w_grid_send_held[...]).astype(BF)

    embed_lent(0)

    def enc_first(i, carry):
        part = pl.ds(pl.multiple_of(i * 512, 512), 512)
        edge_sum[part, :] += dot(enc_hot[part, near : near + 256], enc_lent[...])
        return carry

    lax.fori_loop(0, enc_hot.shape[0] // 512, enc_first, 0)
    embed_lent(1)

    def enc_second(i, carry):
        part = pl.ds(pl.multiple_of(i * 512, 512), 512)
        total = edge_sum[part, :] + dot(enc_hot[part, near + 256 :], enc_lent[...])
        edge_msg[part, :] = silu_of_half(total).astype(BF)
        return carry

    lax.fori_loop(0, enc_hot.shape[0] // 512, enc_second, 0)
    mesh_now[...] = mean(enc_to[...], edge_msg[0 : enc_to.shape[1], :], enc_count[...]).astype(BF)

    def lend(k, picks, values):
        for h in range(2):
            at = h * half
            stacked = jnp.concatenate(
                [values[:, at : at + quarter], values[:, at + quarter : at + half]], axis=0
            )
            mesh_out[k, h] = dot(picks, stacked).astype(BF)
            for dz, dx in FAR_FIRST:
                send(
                    mesh_out.at[k, h, pl.ds(16 * plain_slot(dz, dx), 16)],
                    mesh_got.at[k, h, pl.ds(16 * plain_slot(-dz, -dx), 16)],
                    send_sem.at[2 + 2 * k + h],
                    recv_sem.at[2 + 2 * k + h],
                    (dz, dx),
                )

    def borrow(k, h):
        wait_for(mesh_got.at[k, h, pl.ds(16, 16 * (N_DOM - 1))], recv_sem.at[2 + 2 * k + h])
        got = mesh_got[k, h].astype(F32).reshape(N_DOM, 16, quarter)
        low = got[:, 0:8, :].reshape(N_DOM * 8, quarter)
        high = got[:, 8:16, :].reshape(N_DOM * 8, quarter)
        return jnp.concatenate([low, high], axis=1).astype(BF)

    def messages_of(hots, table, h, unroll):
        at = h * half

        def step(i, carry):
            part = pl.ds(pl.multiple_of(i * 512, 512), 512)
            total = edge_sum[part, at : at + half] + dot(hots[part, 256:512], table)
            edge_msg[part, at : at + half] = silu_of_half(total).astype(BF)
            return carry

        lax.fori_loop(0, hots.shape[0] // 512, step, 0, unroll=unroll)

    for load in loads[3:]:
        load.wait()
    for k in range(2):
        values = dot(mesh_now[...], w_proc_send_held[k]).astype(BF)
        lend(k, lend_hot[0], values)
        mesh_table[0:128, :] = values
        edge_weights(mesh_table, 128, w_proc_edge[k])
        local_sums(mesh_hot, 256, mesh_table[...])
        if k == 0:
            edge_rows(dec_rows, dec_feat, dec_sender, n_mesh, SLOTS_MESH, False)
            sender_hot(dec_rows, dec_hot, n_mesh, N_DOM * SLOTS_MESH)
        else:
            receiver_hot(dec_offset, dec_to, dec_count, dec_block)

            def skip(i, carry):
                part = pl.ds(pl.multiple_of(i * 256, 256), 256)
                mixed[part, :] = dot(grid_latent[part, :], w_skip_held[...])
                return carry

            lax.fori_loop(0, n_grid // 256, skip, 0)
        for h in range(2):
            at = h * half
            messages_of(mesh_hot, borrow(k, h), h, 2)
            mesh_mean[:, at : at + half] = mean(
                mesh_to[...], edge_msg[0 : mesh_to.shape[1], at : at + half], mesh_count[...]
            ).astype(BF)
        update = silu(dot(mesh_mean[...], w_proc_node_held[k]))
        mesh_now[...] = (mesh_now[...].astype(F32) + update).astype(BF)

    lend(2, lend_hot[1], mesh_now[...])
    mesh_table[0:128, :] = mesh_now[...]
    edge_weights(mesh_table, 128, w_dec_edge[...])
    local_sums(dec_hot, 256, mesh_table[...])
    for h in range(2):
        at = h * half
        messages_of(dec_hot, borrow(2, h), h, 1)

        def decode(i, carry):
            part = pl.ds(pl.multiple_of(i * 256, 256), 256)
            grid_mean = mean(dec_to[part, :], edge_msg[:, at : at + half], dec_count[part, :])
            total = mixed[part, :] + dot(grid_mean.astype(BF), w_dec_held[at : at + half, :])
            if h == 0:
                mixed[part, :] = total
            else:
                out[:, part] = dot_turned(w_out_held[...], silu(total).astype(BF)).astype(BF)
            return carry

        lax.fori_loop(0, n_grid // 256, decode, 0)

    wait_for(lists_got.at[pl.ds(1, N_DOM - 1)], lists_sem.at[0])
    wait_for(grid_out.at[pl.ds(0, 256)], send_sem.at[0])
    wait_for(grid_out.at[pl.ds(272, 240)], send_sem.at[1])
    for k in range(3):
        for h in range(2):
            wait_for(mesh_out.at[k, h, pl.ds(16, 16 * (N_DOM - 1))], send_sem.at[2 + 2 * k + h])


def local(
    grid_in,
    w_embed,
    w_grid_send,
    enc_feat,
    w_enc_edge,
    enc_sender,
    enc_offset,
    grid_rows,
    w_proc_send,
    w_proc_edge,
    w_proc_node,
    mesh_feat,
    mesh_sender,
    mesh_offset,
    mesh_rows,
    w_skip,
    w_dec,
    w_dec_edge,
    dec_feat,
    dec_sender,
    dec_offset,
    dec_block,
    dec_rows,
    w_out,
):
    n_grid = grid_in.shape[0]
    width = w_embed.shape[1]
    n_mesh = 128
    enc, mesh, dec = enc_sender.shape[0], mesh_sender.shape[0], dec_sender.shape[0]
    operands = (
        grid_in.T,
        w_embed,
        w_grid_send,
        enc_feat,
        w_enc_edge,
        enc_sender.reshape(1, enc),
        enc_offset.reshape(1, enc),
        grid_rows.T,
        mesh_rows.T,
        dec_rows.T,
        w_proc_send,
        w_proc_edge,
        w_proc_node,
        mesh_feat,
        mesh_sender.reshape(1, mesh),
        mesh_offset.reshape(1, mesh),
        w_skip,
        w_dec,
        w_dec_edge,
        dec_feat,
        dec_sender.reshape(1, dec),
        dec_offset.reshape(1, dec),
        dec_block.reshape(1, dec_block.shape[0]),
        w_out.T,
    )
    whole = pl.BlockSpec(memory_space=pltpu.VMEM)
    far = pl.BlockSpec(memory_space=pl.ANY)
    in_specs = [whole] * len(operands)
    for i in (0, 1, 2, 10, 12, 16, 17, 23):
        in_specs[i] = far
    in_specs[22] = pl.BlockSpec(memory_space=pltpu.SMEM)
    forecast = pl.pallas_call(
        kernel,
        out_shape=jax.ShapeDtypeStruct((w_out.shape[1], n_grid), BF),
        in_specs=in_specs,
        out_specs=whole,
        scratch_shapes=[
            pltpu.VMEM((N_DOM, 1, 128), jnp.int32),
            pltpu.VMEM((N_DOM, 1, 128), jnp.int32),
            pltpu.VMEM((512, 256), BF),
            pltpu.VMEM((512, 256), BF),
            pltpu.VMEM((3, 2, 512, width // 4), BF),
            pltpu.VMEM((3, 2, 512, width // 4), BF),
            pltpu.VMEM((512, 128), F32),
            pltpu.VMEM((512, 128), F32),
            pltpu.VMEM((512, 128), F32),
            pltpu.VMEM((2, 512, 256), BF),
            pltpu.VMEM((8, enc), F32),
            pltpu.VMEM((8, mesh), F32),
            pltpu.VMEM((8, dec), F32),
            pltpu.VMEM((enc, n_grid + 128 + 512), BF),
            pltpu.VMEM((mesh, 512), BF),
            pltpu.VMEM((dec, 512), BF),
            pltpu.VMEM((n_mesh, enc), BF),
            pltpu.VMEM((n_mesh, mesh), BF),
            pltpu.VMEM((n_grid, dec), BF),
            pltpu.VMEM((n_mesh, 128), F32),
            pltpu.VMEM((n_mesh, 128), F32),
            pltpu.VMEM((n_grid, 128), F32),
            pltpu.VMEM((n_grid, width), BF),
            pltpu.VMEM((n_grid + 128, width), BF),
            pltpu.VMEM((256, width), BF),
            pltpu.VMEM((256, width), BF),
            pltpu.VMEM((max(enc, dec), width), F32),
            pltpu.VMEM((max(enc, dec), width), BF),
            pltpu.VMEM((n_mesh, width), BF),
            pltpu.VMEM((n_mesh, width), BF),
            pltpu.VMEM((n_grid, width), F32),
            pltpu.VMEM((256, grid_in.shape[1]), BF),
            pltpu.VMEM(grid_in.shape[::-1], BF),
            pltpu.VMEM(w_embed.shape, BF),
            pltpu.VMEM(w_grid_send.shape, BF),
            pltpu.VMEM(w_proc_send.shape, BF),
            pltpu.VMEM(w_proc_node.shape, BF),
            pltpu.VMEM(w_skip.shape, BF),
            pltpu.VMEM(w_dec.shape, BF),
            pltpu.VMEM(w_out.shape[::-1], BF),
            pltpu.SemaphoreType.DMA((8,)),
            pltpu.SemaphoreType.DMA((2,)),
            pltpu.SemaphoreType.DMA((8,)),
            pltpu.SemaphoreType.DMA((8,)),
        ],
        compiler_params=pltpu.CompilerParams(
            collective_id=0, has_side_effects=True, vmem_limit_bytes=56 * 1024 * 1024
        ),
        name="graph_weather",
    )(*operands)
    return forecast.T


def solution(mesh):
    in_specs = (
        P(("member", "dom"), None),
        P(),
        P(),
        P(None, "dom"),
        P(),
        P("dom"),
        P("dom"),
        P("dom", None),
        P(),
        P(),
        P(),
        P(None, "dom"),
        P("dom"),
        P("dom"),
        P("dom", None),
        P(),
        P(),
        P(),
        P(None, "dom"),
        P("dom"),
        P("dom"),
        P("dom"),
        P("dom", None),
        P(),
    )
    out_specs = P(("member", "dom"), None)
    return jax.shard_map(local, mesh=mesh, in_specs=in_specs, out_specs=out_specs, check_vma=False)
```

time: 72.7 us -> 69.3 us (0.953)
  Pallas kernels: 70.6 us -> 67.2 us
    pallas_call x1, Pallas kernels: 70.6 us -> 67.2 us  [local(): pl.pallas_call(kernel, out_shape=jax.ShapeDtypeStruct((w_out.shape[1], n_...]
where the time goes in v3:
time: 69.3 us; the launch traced here: 69 us
  Pallas kernels  67.2 us (97%)
  local copies, waits for them, and re-layouts  1.83 us (3%)
    pallas_call x1, Pallas kernels, local(): pl.pallas_call(kernel, out_shape=jax.ShapeDtypeStruct((w_out.shape[1], n_...  67.2 us
    unnamed x1, local copies, waits for them, and re-layouts  1.83 us

profile of v3, /device:TPU:56, one launch (start us, length us, event | category | flops | bytes accessed | tf_op | source)
XLA Modules:
  0.0 69.0 jit_solution(15313669242260712194)
XLA Ops:
  0.0 67.2 %graph_weather.1 = bf16[227,1024]{1,0:T(8,128)(2,1)} custom-call(bf16[227,1024]{1,0:T(8,128)(2,1)} %bitcast.14, bf16[227,512]{1,0:T(8,128)(2,1)} %w_embed.1, bf16[512,512]{1,0:T(8,128)(2,1)} %w_grid_send.1, bf16[4,2048]{1,0:T(4,128)(2,1)} %enc_feat.1, bf16[4,512]{1,0:T(4,128)(2,1)} %w_enc_edge.1, s32[1,2048]{1,0:T(1,128)} %bitcast.18, s32[1,2048]{1,0:T(1,128)} %bitcast.19, ...), custom_call_target="tpu_custom_call" | custom-call | tf_op jit(solution)/shard_map/graph_weather/pallas_call | solution.py:510
  67.2 1.8 %copy.26 = bf16[1024,227]{0,1:T(8,128)(2,1)} copy(bf16[1024,227]{0,1:T(8,128)(2,1)} %bitcast.13) | data formatting | bytes 929792

commit v4 on v3

v4 whole, which is shorter than its diff:
```python
import jax
import jax.numpy as jnp
from jax import lax
from jax.experimental import pallas as pl
from jax.experimental.pallas import tpu as pltpu
from jax.sharding import PartitionSpec as P

N_Z, N_X = 8, 4
N_DOM = N_Z * N_X
SLOTS_GRID = 16
SLOTS_MESH = 8
BF = jnp.bfloat16
F32 = jnp.float32
N_LOADS = 24


def silu_of_half(half):
    return half + half * jnp.tanh(half)


def silu(v):
    return silu_of_half(0.5 * v)


def dot(a, b):
    return jnp.dot(a, b, preferred_element_type=F32)


def dot_turned(a, b):
    return lax.dot_general(a, b, (((1,), (1,)), ((), ())), preferred_element_type=F32)


def lanes(shape):
    return lax.broadcasted_iota(jnp.int32, shape, 1).astype(F32)


def rows(shape):
    return lax.broadcasted_iota(jnp.int32, shape, 0).astype(F32)


def hot(index, offset, value=1.0):
    return jnp.where(index == lanes(index.shape) + offset, value, 0.0).astype(BF)


def hops(offset):
    dz, dx = offset
    return min(dz, N_Z - dz) + min(dx, N_X - dx)


OFFSETS = [(dz, dx) for dz in range(N_Z) for dx in range(N_X) if (dz, dx) != (0, 0)]
FAR_FIRST = sorted(OFFSETS, key=lambda offset: -hops(offset))


def slot(dz, dx):
    return (dz % N_Z) * N_X + dx % N_X


def kernel(*refs):
    far, out, held = refs[0:N_LOADS], refs[N_LOADS], refs[N_LOADS + 1 : 2 * N_LOADS + 1]
    (
        grid_list,
        mesh_list,
        dec_list,
        grid_in,
        w_embed,
        w_grid_send,
        enc_sender,
        enc_feat,
        w_enc_edge,
        enc_offset,
        mesh_sender,
        mesh_feat,
        w_proc_edge,
        mesh_offset,
        w_proc_send,
        w_proc_node,
        dec_sender,
        dec_feat,
        w_dec_edge,
        dec_offset,
        dec_block,
        w_skip,
        w_dec,
        w_out,
    ) = held
    (
        lists_out,
        lists_got,
        rows_out,
        rows_got,
        lend_grid,
        lend_mesh,
        lend_dec,
        lend_hot,
        enc_rows,
        mesh_rows,
        dec_rows,
        enc_hot,
        mesh_hot,
        dec_hot,
        enc_to,
        mesh_to,
        dec_to,
        enc_count,
        mesh_count,
        block_count,
        dec_count,
        running,
        grid_turned,
        grid_latent,
        enc_table,
        enc_lent,
        mesh_table,
        edge_sum,
        edge_msg,
        dec_msg,
        mesh_now,
        mesh_mean,
        grid_mean,
        mixed,
        rank,
        order,
        keep,
        last,
        load_sem,
        lists_sem,
        send_sem,
        recv_sem,
    ) = refs[2 * N_LOADS + 1 :]
    me = lax.axis_index("dom")
    me_z, me_x = me // N_X, lax.rem(me, N_X)
    width = w_embed.shape[1]
    half = width // 2
    quarter = width // 4
    channels, n_grid = grid_in.shape
    n_mesh = mesh_to.shape[0]
    n_edge_blocks = dec_block.shape[1]
    n_blocks = n_grid // 128
    near = n_grid + 128

    def peer(dz, dx):
        return lax.rem(me_z + dz, N_Z) * N_X + lax.rem(me_x + dx, N_X)

    def send(source, target, out_sem, in_sem, offset):
        pltpu.make_async_remote_copy(
            src_ref=source,
            dst_ref=target,
            send_sem=out_sem,
            recv_sem=in_sem,
            device_id={"dom": peer(*offset)},
            device_id_type=pl.DeviceIdType.MESH,
        ).start()

    def wait_for(part, sem):
        pltpu.make_async_copy(part, part, sem).wait()

    barrier = pltpu.get_barrier_semaphore()
    for offset in FAR_FIRST:
        pl.semaphore_signal(
            barrier,
            inc=1,
            device_id={"dom": peer(*offset)},
            device_id_type=pl.DeviceIdType.MESH,
        )

    loads = [
        pltpu.make_async_copy(source, target, load_sem.at[i])
        for i, (source, target) in enumerate(zip(far, held))
    ]
    for load in loads:
        load.start()

    lists_got[0:1] = jnp.zeros((1, 1, 128), jnp.int32)
    for x in range(4):
        for h in range(2):
            rows_got[x, h, 0:16, :] = jnp.zeros((16, quarter), BF)

    for load in loads[0:3]:
        load.wait()
    slots = jnp.concatenate([grid_list[...], mesh_list[...], dec_list[...]], axis=0).astype(F32)
    slots = jnp.concatenate([slots, jnp.zeros((N_DOM, 96), F32)], axis=1)
    slots = jnp.transpose(jnp.concatenate([slots, jnp.zeros((96, 128), F32)], axis=0))
    for p in range(N_DOM):
        lists_out[p] = slots[p : p + 1, :].astype(jnp.int32)

    pl.semaphore_wait(barrier, N_DOM - 1)
    for dz, dx in FAR_FIRST:
        send(
            lists_out.at[pl.ds(peer(dz, dx), 1)],
            lists_got.at[pl.ds(slot(-dz, -dx), 1)],
            lists_sem.at[0],
            lists_sem.at[1],
            (dz, dx),
        )

    for load in loads[3:6]:
        load.wait()
    grid_turned[:, channels - channels % 128 :] = jnp.zeros((n_grid, 128), BF)
    grid_turned[:, 0:channels] = jnp.transpose(grid_in[...])

    def embed(i, carry):
        part = pl.ds(pl.multiple_of(i * 512, 512), 512)
        latent = silu(dot(grid_turned[part, 0:channels], w_embed[...])).astype(BF)
        grid_latent[part, :] = latent
        enc_table[part, :] = dot(latent, w_grid_send[...]).astype(BF)
        return carry

    lax.fori_loop(0, n_grid // 512, embed, 0)

    def edge_rows(scratch, feat, sender, n_local, n_slots):
        value = sender[...]
        shifted = jnp.maximum(value - n_local, 0)
        giver = shifted >> (n_slots.bit_length() - 1)
        listed = shifted & (n_slots - 1)
        dz = ((giver >> 2) - me_z) & (N_Z - 1)
        dx = ((giver & (N_X - 1)) - me_x) & (N_X - 1)
        lent = ((listed >> 3) << 8) + ((dz * N_X + dx) << 3) + (listed & 7)
        local = value < n_local
        scratch[...] = jnp.zeros_like(scratch)
        scratch[0:4, :] = 0.5 * feat[...].astype(F32)
        scratch[4:5, :] = jnp.where(local, value, -1).astype(F32)
        scratch[5:6, :] = jnp.where(local, -1, lent).astype(F32)

    def sender_hot(scratch, hots, n_local, n_lent):
        def step(i, carry):
            part = pl.ds(pl.multiple_of(i * 128, 128), 128)
            turned = jnp.transpose(
                jnp.concatenate([scratch[:, part], jnp.zeros((120, 128), F32)], axis=0)
            )
            local = jnp.broadcast_to(turned[:, 4:5], (128, 128))
            lent = jnp.broadcast_to(turned[:, 5:6], (128, 128))
            for j in range(n_local // 128):
                hots[part, 128 * j : 128 * j + 128] = hot(local, 128.0 * j, 0.5)
            hots[part, n_local : n_local + 128] = turned.astype(BF)
            for j in range(n_lent // 128):
                at = n_local + 128 + 128 * j
                hots[part, at : at + 128] = hot(lent, 128.0 * j, 0.5)
            return carry

        lax.fori_loop(0, hots.shape[0] // 128, step, 0, unroll=8)

    def receiver_hot(target, hots, count):
        n_rows = hots.shape[0]
        count[...] = jnp.zeros_like(count)

        def step(i, carry):
            part = pl.ds(pl.multiple_of(i * 128, 128), 128)
            wanted = jnp.broadcast_to(target[:, part].astype(F32), (n_rows, 128))
            same = jnp.where(wanted == rows((n_rows, 128)), 1.0, 0.0)
            hots[:, part] = same.astype(BF)
            count[...] += same
            return carry

        lax.fori_loop(0, hots.shape[1] // 128, step, 0, unroll=4)
        total = jnp.sum(count[...], axis=1, keepdims=True)
        count[...] = jnp.broadcast_to(1.0 / jnp.maximum(total, 1.0), count.shape)

    def edge_weights(table, at, w_edge):
        table[at : at + 128, :] = jnp.zeros((128, width), BF)
        table[at : at + 4, :] = w_edge

    def mean(hots, messages, count):
        columns = messages.shape[1]
        return dot(hots, messages) * jnp.concatenate([count] * (columns // 128), axis=1)

    for load in loads[6:10]:
        load.wait()
    edge_rows(enc_rows, enc_feat, enc_sender, n_grid, SLOTS_GRID)
    sender_hot(enc_rows, enc_hot, n_grid, N_DOM * SLOTS_GRID)
    edge_weights(enc_table, n_grid, w_enc_edge[...])

    def ship(x, h):
        for dz, dx in FAR_FIRST:
            send(
                rows_out.at[x, h, pl.ds(16 * slot(dz, dx), 16)],
                rows_got.at[x, h, pl.ds(16 * slot(-dz, -dx), 16)],
                send_sem.at[2 * x + h],
                recv_sem.at[2 * x + h],
                (dz, dx),
            )

    def arrive(x, h):
        wait_for(rows_got.at[x, h, pl.ds(16, 16 * (N_DOM - 1))], recv_sem.at[2 * x + h])
        got = rows_got[x, h].astype(F32).reshape(N_DOM, 16, quarter)
        low = got[:, 0:8, :].reshape(N_DOM * 8, quarter)
        high = got[:, 8:16, :].reshape(N_DOM * 8, quarter)
        return jnp.concatenate([low, high], axis=1).astype(BF)

    wait_for(lists_got.at[pl.ds(1, N_DOM - 1)], lists_sem.at[1])
    listed = lists_got[:, 0, :].astype(F32)
    listed = jnp.transpose(jnp.concatenate([listed, jnp.zeros((96, 128), F32)], axis=0))
    for h in range(2):
        for q in range(N_DOM):
            lend_grid[h, 8 * q : 8 * q + 8, :] = jnp.broadcast_to(
                listed[8 * h : 8 * h + 8, q : q + 1], (8, 128)
            )
        picks = jnp.concatenate(
            [hot(lend_grid[h], 128.0 * j) for j in range(n_grid // 128)], axis=1
        )
        lent = dot(picks, grid_turned[...]).reshape(N_DOM, 8, 2 * quarter)
        lent = jnp.concatenate([lent[:, :, 0:quarter], lent[:, :, quarter:]], axis=1)
        rows_out[0, h] = lent.reshape(16 * N_DOM, quarter).astype(BF)
        ship(0, h)

    for q in range(N_DOM):
        for lent, first in ((lend_mesh, 16), (lend_dec, 24)):
            column = jnp.broadcast_to(listed[first : first + 8, q : q + 1], (8, 128))
            lent[16 * q : 16 * q + 8, :] = column
            lent[16 * q + 8 : 16 * q + 16, :] = column + 128.0
    for k, lent in enumerate((lend_mesh, lend_dec)):
        lend_hot[k] = jnp.concatenate([hot(lent[...], 0.0), hot(lent[...], 128.0)], axis=1)

    def local_sums(hots, columns, table):
        def step(i, carry):
            part = pl.ds(pl.multiple_of(i * 1024, 1024), 1024)
            edge_sum[part, :] = dot(hots[part, 0:columns], table)
            return carry

        lax.fori_loop(0, hots.shape[0] // 1024, step, 0)

    local_sums(enc_hot, near, enc_table[...])
    receiver_hot(enc_offset, enc_to, enc_count)

    def embed_lent(h):
        latent = silu(dot(arrive(0, h)[:, 0:channels], w_embed[...])).astype(BF)
        enc_lent[...] = dot(latent, w_grid_send[...]).astype(BF)

    embed_lent(0)

    def enc_first(i, carry):
        part = pl.ds(pl.multiple_of(i * 1024, 1024), 1024)
        edge_sum[part, :] += dot(enc_hot[part, near : near + 256], enc_lent[...])
        return carry

    lax.fori_loop(0, enc_hot.shape[0] // 1024, enc_first, 0)
    for load in loads[10:]:
        load.wait()
    embed_lent(1)

    def enc_second(i, carry):
        part = pl.ds(pl.multiple_of(i * 1024, 1024), 1024)
        total = edge_sum[part, :] + dot(enc_hot[part, near + 256 :], enc_lent[...])
        edge_msg[part, :] = silu_of_half(total).astype(BF)
        return carry

    lax.fori_loop(0, enc_hot.shape[0] // 1024, enc_second, 0)
    mesh_now[...] = mean(enc_to[...], edge_msg[0 : enc_to.shape[1], :], enc_count[...]).astype(BF)

    def lend(x, picks, values):
        for h in range(2):
            at = h * half
            stacked = jnp.concatenate(
                [values[:, at : at + quarter], values[:, at + quarter : at + half]], axis=0
            )
            rows_out[x, h] = dot(picks, stacked).astype(BF)
            ship(x, h)

    def messages_of(hots, table, h, by_block=False):
        at = h * half

        def step(i, carry):
            part = pl.ds(pl.multiple_of(i * 1024, 1024), 1024)
            total = edge_sum[part, at : at + half] + dot(hots[part, 256:512], table)
            message = silu_of_half(total).astype(BF)
            if by_block:
                blocks = pl.ds(pl.multiple_of(i * 8, 8), 8)
                dec_msg[blocks, :, at : at + half] = message.reshape(8, 128, half)
            else:
                edge_msg[part, at : at + half] = message
            return carry

        lax.fori_loop(0, hots.shape[0] // 1024, step, 0)

    def sort_blocks():
        def rank_of(b, carry):
            own = dec_block[0, b] * 32 + b
            below = jnp.int32(0)
            for other in range(n_edge_blocks):
                below += jnp.where(dec_block[0, other] * 32 + other < own, 1, 0)
            rank[b] = below
            return carry

        lax.fori_loop(0, n_edge_blocks, rank_of, 0)

        def block_at(t, carry):
            found = jnp.int32(0)
            for b in range(n_edge_blocks):
                found += jnp.where(rank[b] == t, b, 0)
            order[t] = found
            return carry

        lax.fori_loop(0, n_edge_blocks, block_at, 0)

        def kept(t, carry):
            same = dec_block[0, order[t]] == dec_block[0, order[jnp.maximum(t - 1, 0)]]
            keep[t] = jnp.where(same, 1, 0)
            return carry

        lax.fori_loop(0, n_edge_blocks, kept, 0)

        def last_of(g, carry):
            before, until = jnp.int32(0), jnp.int32(0)
            for b in range(n_edge_blocks):
                before += jnp.where(dec_block[0, b] < g, 1, 0)
                until += jnp.where(dec_block[0, b] <= g, 1, 0)
            last[g] = jnp.where(until > before, until, 0)
            return carry

        lax.fori_loop(0, n_blocks, last_of, 0)

    def dec_receivers():
        def step(b, carry):
            part = pl.ds(pl.multiple_of(b * 128, 128), 128)
            wanted = jnp.broadcast_to(dec_offset[:, part].astype(F32), (128, 128))
            same = jnp.where(wanted == rows((128, 128)), 1.0, 0.0)
            dec_to[b] = same.astype(BF)
            block_count[b] = jnp.broadcast_to(
                jnp.sum(same, axis=1, keepdims=True), (128, 128)
            )
            return carry

        lax.fori_loop(0, n_edge_blocks, step, 0, unroll=4)
        total = jnp.zeros((128, 128), F32)
        running[0] = jnp.zeros((128, width), F32)
        for t in range(n_edge_blocks):
            total = block_count[order[t]] + keep[t].astype(F32) * total
            running[t + 1, :, 0:128] = total
        for g in range(n_blocks):
            count = running[last[g], :, 0:128]
            dec_count[128 * g : 128 * g + 128, :] = 1.0 / jnp.maximum(count, 1.0)

    for k in range(2):
        values = dot(mesh_now[...], w_proc_send[k]).astype(BF)
        lend(1 + k, lend_hot[0], values)
        mesh_table[0:128, :] = values
        edge_weights(mesh_table, 128, w_proc_edge[k])
        if k == 0:
            edge_rows(mesh_rows, mesh_feat, mesh_sender, n_mesh, SLOTS_MESH)
            sender_hot(mesh_rows, mesh_hot, n_mesh, N_DOM * SLOTS_MESH)
            receiver_hot(mesh_offset, mesh_to, mesh_count)
            sort_blocks()
        local_sums(mesh_hot, 256, mesh_table[...])
        if k == 1:
            edge_rows(dec_rows, dec_feat, dec_sender, n_mesh, SLOTS_MESH)
            sender_hot(dec_rows, dec_hot, n_mesh, N_DOM * SLOTS_MESH)
            dec_receivers()
        for h in range(2):
            at = h * half
            messages_of(mesh_hot, arrive(1 + k, h), h)
            mesh_mean[:, at : at + half] = mean(
                mesh_to[...], edge_msg[0 : mesh_to.shape[1], at : at + half], mesh_count[...]
            ).astype(BF)
        update = silu(dot(mesh_mean[...], w_proc_node[k]))
        mesh_now[...] = (mesh_now[...].astype(F32) + update).astype(BF)

    lend(3, lend_hot[1], mesh_now[...])
    mesh_table[0:128, :] = mesh_now[...]
    edge_weights(mesh_table, 128, w_dec_edge[...])
    local_sums(dec_hot, 256, mesh_table[...])
    mixed[...] = dot(grid_latent[...], w_skip[...])
    for h in range(2):
        at = h * half
        messages_of(dec_hot, arrive(3, h), h, True)
        total = jnp.zeros((128, half), F32)
        for t in range(n_edge_blocks):
            block = dot(dec_to[order[t]], dec_msg[order[t], :, at : at + half])
            total = block + keep[t].astype(F32) * total
            running[t + 1, :, at : at + half] = total
        for g in range(n_blocks):
            count = dec_count[128 * g : 128 * g + 128, :]
            grid_mean[128 * g : 128 * g + 128, :] = (
                running[last[g], :, at : at + half] * jnp.concatenate([count] * (half // 128), axis=1)
            ).astype(BF)
        total = mixed[...] + dot(grid_mean[...], w_dec[at : at + half, :])
        if h == 0:
            mixed[...] = total
        else:
            out[...] = dot_turned(w_out[...], silu(total).astype(BF)).astype(BF)

    wait_for(lists_got.at[pl.ds(1, N_DOM - 1)], lists_sem.at[0])
    for x in range(4):
        for h in range(2):
            wait_for(rows_out.at[x, h, pl.ds(16, 16 * (N_DOM - 1))], send_sem.at[2 * x + h])


def local(
    grid_in,
    w_embed,
    w_grid_send,
    enc_feat,
    w_enc_edge,
    enc_sender,
    enc_offset,
    grid_rows,
    w_proc_send,
    w_proc_edge,
    w_proc_node,
    mesh_feat,
    mesh_sender,
    mesh_offset,
    mesh_rows,
    w_skip,
    w_dec,
    w_dec_edge,
    dec_feat,
    dec_sender,
    dec_offset,
    dec_block,
    dec_rows,
    w_out,
):
    n_grid = grid_in.shape[0]
    width = w_embed.shape[1]
    n_mesh = 128
    enc, mesh, dec = enc_sender.shape[0], mesh_sender.shape[0], dec_sender.shape[0]
    operands = (
        grid_rows.T,
        mesh_rows.T,
        dec_rows.T,
        grid_in.T,
        w_embed,
        w_grid_send,
        enc_sender.reshape(1, enc),
        enc_feat,
        w_enc_edge,
        enc_offset.reshape(1, enc),
        mesh_sender.reshape(1, mesh),
        mesh_feat,
        w_proc_edge,
        mesh_offset.reshape(1, mesh),
        w_proc_send,
        w_proc_node,
        dec_sender.reshape(1, dec),
        dec_feat,
        w_dec_edge,
        dec_offset.reshape(1, dec),
        dec_block.reshape(1, dec_block.shape[0]),
        w_skip,
        w_dec,
        w_out.T,
    )
    held = [
        pltpu.SMEM(operand.shape, operand.dtype)
        if i == 20
        else pltpu.VMEM(operand.shape, operand.dtype)
        for i, operand in enumerate(operands)
    ]
    most = max(enc, dec)
    forecast = pl.pallas_call(
        kernel,
        out_shape=pltpu.VMEM((w_out.shape[1], n_grid), BF),
        in_specs=[pl.BlockSpec(memory_space=pl.ANY)] * len(operands),
        out_specs=pl.BlockSpec(memory_space=pltpu.VMEM),
        scratch_shapes=held
        + [
            pltpu.VMEM((N_DOM, 1, 128), jnp.int32),
            pltpu.VMEM((N_DOM, 1, 128), jnp.int32),
            pltpu.VMEM((4, 2, 512, width // 4), BF),
            pltpu.VMEM((4, 2, 512, width // 4), BF),
            pltpu.VMEM((2, 256, 128), F32),
            pltpu.VMEM((512, 128), F32),
            pltpu.VMEM((512, 128), F32),
            pltpu.VMEM((2, 512, 256), BF),
            pltpu.VMEM((8, enc), F32),
            pltpu.VMEM((8, mesh), F32),
            pltpu.VMEM((8, dec), F32),
            pltpu.VMEM((enc, n_grid + 128 + 512), BF),
            pltpu.VMEM((mesh, 512), BF),
            pltpu.VMEM((dec, 512), BF),
            pltpu.VMEM((n_mesh, enc), BF),
            pltpu.VMEM((n_mesh, mesh), BF),
            pltpu.VMEM((dec // 128, 128, 128), BF),
            pltpu.VMEM((n_mesh, 128), F32),
            pltpu.VMEM((n_mesh, 128), F32),
            pltpu.VMEM((dec // 128, 128, 128), F32),
            pltpu.VMEM((n_grid, 128), F32),
            pltpu.VMEM((dec // 128 + 1, 128, width), F32),
            pltpu.VMEM((n_grid, 256), BF),
            pltpu.VMEM((n_grid, width), BF),
            pltpu.VMEM((n_grid + 128, width), BF),
            pltpu.VMEM((256, width), BF),
            pltpu.VMEM((256, width), BF),
            pltpu.VMEM((most, width), F32),
            pltpu.VMEM((max(enc, mesh), width), BF),
            pltpu.VMEM((dec // 128, 128, width), BF),
            pltpu.VMEM((n_mesh, width), BF),
            pltpu.VMEM((n_mesh, width), BF),
            pltpu.VMEM((n_grid, width // 2), BF),
            pltpu.VMEM((n_grid, width), F32),
            pltpu.SMEM((dec // 128,), jnp.int32),
            pltpu.SMEM((dec // 128,), jnp.int32),
            pltpu.SMEM((dec // 128,), jnp.int32),
            pltpu.SMEM((n_grid // 128,), jnp.int32),
            pltpu.SemaphoreType.DMA((N_LOADS,)),
            pltpu.SemaphoreType.DMA((2,)),
            pltpu.SemaphoreType.DMA((8,)),
            pltpu.SemaphoreType.DMA((8,)),
        ],
        compiler_params=pltpu.CompilerParams(
            collective_id=0, has_side_effects=True, vmem_limit_bytes=56 * 1024 * 1024
        ),
        name="graph_weather",
    )(*operands)
    return forecast.T


def solution(mesh):
    in_specs = (
        P(("member", "dom"), None),
        P(),
        P(),
        P(None, "dom"),
        P(),
        P("dom"),
        P("dom"),
        P("dom", None),
        P(),
        P(),
        P(),
        P(None, "dom"),
        P("dom"),
        P("dom"),
        P("dom", None),
        P(),
        P(),
        P(),
        P(None, "dom"),
        P("dom"),
        P("dom"),
        P("dom"),
        P("dom", None),
        P(),
    )
    out_specs = P(("member", "dom"), None)
    return jax.shard_map(local, mesh=mesh, in_specs=in_specs, out_specs=out_specs, check_vma=False)
```

time: 69.3 us -> 59.3 us (0.86)
  Pallas kernels: 67.2 us -> 58.2 us
  local copies, waits for them, and re-layouts: 1.83 us -> 0.78 us
    pallas_call x1, Pallas kernels: 67.2 us -> 58.2 us  [local(): pl.pallas_call(kernel, out_shape=pltpu.VMEM((w_out.shape[1], n_grid), BF)...]
    unnamed x1, local copies, waits for them, and re-layouts: 1.83 us -> 0.78 us
where the time goes in v4:
time: 59.3 us; the launch traced here: 59 us
  Pallas kernels  58.2 us (98%)
  local copies, waits for them, and re-layouts  0.78 us (1%)
    pallas_call x1, Pallas kernels, local(): pl.pallas_call(kernel, out_shape=pltpu.VMEM((w_out.shape[1], n_grid), BF)...  58.2 us

profile of v4, /device:TPU:56, one launch (start us, length us, event | category | flops | bytes accessed | tf_op | source)
XLA Modules:
  0.0 59.0 jit_solution(5042321872950131602)
XLA Ops:
  0.0 58.2 %graph_weather.1 = bf16[227,1024]{1,0:T(8,128)(2,1)S(1)} custom-call(s32[16,32]{1,0:T(8,128)} %bitcast.18, s32[8,32]{1,0:T(8,128)} %bitcast.21, s32[8,32]{1,0:T(8,128)} %bitcast.22, bf16[227,1024]{1,0:T(8,128)(2,1)} %bitcast.14, bf16[227,512]{1,0:T(8,128)(2,1)} %refs_4_.1, bf16[512,512]{1,0:T(8,128)(2,1)} %refs_5_.1, s32[1,2048]{1,0:T(1,128)} %bitcast.19, ...), custom_call_target="tpu_custom_call" | custom-call | tf_op jit(solution)/shard_map/graph_weather/pallas_call | solution.py:549
  58.2 0.8 %copy.26 = bf16[1024,227]{0,1:T(8,128)(2,1)} copy(bf16[1024,227]{0,1:T(8,128)(2,1)S(1)} %bitcast.13) | data formatting | bytes 929792

commit v5 on v4

--- a/solution.py
+++ b/solution.py
@@ -88,6 +88,8 @@
         lists_got,
         rows_out,
         rows_got,
+        wide_out,
+        wide_got,
         lend_grid,
         lend_mesh,
         lend_dec,
@@ -112,10 +114,8 @@
         enc_lent,
         mesh_table,
         edge_sum,
-        edge_msg,
         dec_msg,
         mesh_now,
-        mesh_mean,
         grid_mean,
         mixed,
         rank,
@@ -171,9 +171,10 @@
         load.start()
 
     lists_got[0:1] = jnp.zeros((1, 1, 128), jnp.int32)
-    for x in range(4):
+    for x in range(2):
         for h in range(2):
             rows_got[x, h, 0:16, :] = jnp.zeros((16, quarter), BF)
+        wide_got[x, 0:16, :] = jnp.zeros((16, half), BF)
 
     for load in loads[0:3]:
         load.wait()
@@ -274,17 +275,21 @@
             send(
                 rows_out.at[x, h, pl.ds(16 * slot(dz, dx), 16)],
                 rows_got.at[x, h, pl.ds(16 * slot(-dz, -dx), 16)],
-                send_sem.at[2 * x + h],
-                recv_sem.at[2 * x + h],
+                send_sem.at[4 * x + h],
+                recv_sem.at[4 * x + h],
                 (dz, dx),
             )
 
+    def beside(values):
+        columns = values.shape[1]
+        got = values.astype(F32).reshape(N_DOM, 16, columns)
+        low = got[:, 0:8, :].reshape(N_DOM * 8, columns)
+        high = got[:, 8:16, :].reshape(N_DOM * 8, columns)
+        return jnp.concatenate([low, high], axis=1).astype(BF)
+
     def arrive(x, h):
-        wait_for(rows_got.at[x, h, pl.ds(16, 16 * (N_DOM - 1))], recv_sem.at[2 * x + h])
-        got = rows_got[x, h].astype(F32).reshape(N_DOM, 16, quarter)
-        low = got[:, 0:8, :].reshape(N_DOM * 8, quarter)
-        high = got[:, 8:16, :].reshape(N_DOM * 8, quarter)
-        return jnp.concatenate([low, high], axis=1).astype(BF)
+        wait_for(rows_got.at[x, h, pl.ds(16, 16 * (N_DOM - 1))], recv_sem.at[4 * x + h])
+        return beside(rows_got[x, h])
 
     wait_for(lists_got.at[pl.ds(1, N_DOM - 1)], lists_sem.at[1])
     listed = lists_got[:, 0, :].astype(F32)
@@ -327,49 +332,37 @@
 
     embed_lent(0)
 
-    def enc_first(i, carry):
-        part = pl.ds(pl.multiple_of(i * 1024, 1024), 1024)
+    for i in range(enc_hot.shape[0] // 1024):
+        part = pl.ds(i * 1024, 1024)
         edge_sum[part, :] += dot(enc_hot[part, near : near + 256], enc_lent[...])
-        return carry
-
-    lax.fori_loop(0, enc_hot.shape[0] // 1024, enc_first, 0)
     for load in loads[10:]:
         load.wait()
     embed_lent(1)
 
-    def enc_second(i, carry):
-        part = pl.ds(pl.multiple_of(i * 1024, 1024), 1024)
+    summed = jnp.zeros((n_mesh, width), F32)
+    for i in range(enc_hot.shape[0] // 1024):
+        part = pl.ds(i * 1024, 1024)
         total = edge_sum[part, :] + dot(enc_hot[part, near + 256 :], enc_lent[...])
-        edge_msg[part, :] = silu_of_half(total).astype(BF)
-        return carry
-
-    lax.fori_loop(0, enc_hot.shape[0] // 1024, enc_second, 0)
-    mesh_now[...] = mean(enc_to[...], edge_msg[0 : enc_to.shape[1], :], enc_count[...]).astype(BF)
-
-    def lend(x, picks, values):
-        for h in range(2):
-            at = h * half
-            stacked = jnp.concatenate(
-                [values[:, at : at + quarter], values[:, at + quarter : at + half]], axis=0
-            )
-            rows_out[x, h] = dot(picks, stacked).astype(BF)
-            ship(x, h)
-
-    def messages_of(hots, table, h, by_block=False):
+        summed += dot(enc_to[:, part], silu_of_half(total).astype(BF))
+    mesh_now[...] = (summed * jnp.concatenate([enc_count[...]] * 4, axis=1)).astype(BF)
+
+    def lend(x, h, picks, values):
+        stacked = jnp.concatenate([values[:, 0:quarter], values[:, quarter:]], axis=0)
+        rows_out[x, h] = dot(picks, stacked).astype(BF)
+        ship(x, h)
+
+    def messages_of(hots, table, h):
         at = h * half
 
-        def step(i, carry):
-            part = pl.ds(pl.multiple_of(i * 1024, 1024), 1024)
+        def step(i):
+            part = pl.ds(i * 1024, 1024)
             total = edge_sum[part, at : at + half] + dot(hots[part, 256:512], table)
             message = silu_of_half(total).astype(BF)
-            if by_block:
-                blocks = pl.ds(pl.multiple_of(i * 8, 8), 8)
-                dec_msg[blocks, :, at : at + half] = message.reshape(8, 128, half)
-            else:
-                edge_msg[part, at : at + half] = message
-            return carry
-
-        lax.fori_loop(0, hots.shape[0] // 1024, step, 0)
+            blocks = pl.ds(i * 8, 8)
+            dec_msg[blocks, :, at : at + half] = message.reshape(8, 128, half)
+
+        for i in range(hots.shape[0] // 1024):
+            step(i)
 
     def sort_blocks():
         def rank_of(b, carry):
@@ -431,7 +424,16 @@
 
     for k in range(2):
         values = dot(mesh_now[...], w_proc_send[k]).astype(BF)
-        lend(1 + k, lend_hot[0], values)
+        stacked = jnp.concatenate([values[:, 0:half], values[:, half:]], axis=0)
+        wide_out[k] = dot(lend_hot[0], stacked).astype(BF)
+        for dz, dx in FAR_FIRST:
+            send(
+                wide_out.at[k, pl.ds(16 * slot(dz, dx), 16)],
+                wide_got.at[k, pl.ds(16 * slot(-dz, -dx), 16)],
+                send_sem.at[2 + k],
+                recv_sem.at[2 + k],
+                (dz, dx),
+            )
         mesh_table[0:128, :] = values
         edge_weights(mesh_table, 128, w_proc_edge[k])
         if k == 0:
@@ -444,23 +446,22 @@
             edge_rows(dec_rows, dec_feat, dec_sender, n_mesh, SLOTS_MESH)
             sender_hot(dec_rows, dec_hot, n_mesh, N_DOM * SLOTS_MESH)
             dec_receivers()
-        for h in range(2):
-            at = h * half
-            messages_of(mesh_hot, arrive(1 + k, h), h)
-            mesh_mean[:, at : at + half] = mean(
-                mesh_to[...], edge_msg[0 : mesh_to.shape[1], at : at + half], mesh_count[...]
-            ).astype(BF)
-        update = silu(dot(mesh_mean[...], w_proc_node[k]))
+        wait_for(wide_got.at[k, pl.ds(16, 16 * (N_DOM - 1))], recv_sem.at[2 + k])
+        total = edge_sum[0 : mesh_hot.shape[0], :] + dot(mesh_hot[:, 256:512], beside(wide_got[k]))
+        message = silu_of_half(total).astype(BF)
+        mesh_mean = mean(mesh_to[...], message, mesh_count[...]).astype(BF)
+        update = silu(dot(mesh_mean, w_proc_node[k]))
         mesh_now[...] = (mesh_now[...].astype(F32) + update).astype(BF)
 
-    lend(3, lend_hot[1], mesh_now[...])
+    for h in range(2):
+        lend(1, h, lend_hot[1], mesh_now[:, h * half : h * half + half])
     mesh_table[0:128, :] = mesh_now[...]
     edge_weights(mesh_table, 128, w_dec_edge[...])
     local_sums(dec_hot, 256, mesh_table[...])
     mixed[...] = dot(grid_latent[...], w_skip[...])
     for h in range(2):
         at = h * half
-        messages_of(dec_hot, arrive(3, h), h, True)
+        messages_of(dec_hot, arrive(1, h), h)
         total = jnp.zeros((128, half), F32)
         for t in range(n_edge_blocks):
             block = dot(dec_to[order[t]], dec_msg[order[t], :, at : at + half])
@@ -478,9 +479,10 @@
             out[...] = dot_turned(w_out[...], silu(total).astype(BF)).astype(BF)
 
     wait_for(lists_got.at[pl.ds(1, N_DOM - 1)], lists_sem.at[0])
-    for x in range(4):
+    for x in range(2):
         for h in range(2):
-            wait_for(rows_out.at[x, h, pl.ds(16, 16 * (N_DOM - 1))], send_sem.at[2 * x + h])
+            wait_for(rows_out.at[x, h, pl.ds(16, 16 * (N_DOM - 1))], send_sem.at[4 * x + h])
+        wait_for(wide_out.at[x, pl.ds(16, 16 * (N_DOM - 1))], send_sem.at[2 + x])
 
 
 def local(
@@ -555,8 +557,10 @@
         + [
             pltpu.VMEM((N_DOM, 1, 128), jnp.int32),
             pltpu.VMEM((N_DOM, 1, 128), jnp.int32),
-            pltpu.VMEM((4, 2, 512, width // 4), BF),
-            pltpu.VMEM((4, 2, 512, width // 4), BF),
+            pltpu.VMEM((2, 2, 512, width // 4), BF),
+            pltpu.VMEM((2, 2, 512, width // 4), BF),
+            pltpu.VMEM((2, 512, width // 2), BF),
+            pltpu.VMEM((2, 512, width // 2), BF),
             pltpu.VMEM((2, 256, 128), F32),
             pltpu.VMEM((512, 128), F32),
             pltpu.VMEM((512, 128), F32),
@@ -581,9 +585,7 @@
             pltpu.VMEM((256, width), BF),
             pltpu.VMEM((256, width), BF),
             pltpu.VMEM((most, width), F32),
-            pltpu.VMEM((max(enc, mesh), width), BF),
             pltpu.VMEM((dec // 128, 128, width), BF),
-            pltpu.VMEM((n_mesh, width), BF),
             pltpu.VMEM((n_mesh, width), BF),
             pltpu.VMEM((n_grid, width // 2), BF),
             pltpu.VMEM((n_grid, width), F32),
@@ -593,8 +595,8 @@
             pltpu.SMEM((n_grid // 128,), jnp.int32),
             pltpu.SemaphoreType.DMA((N_LOADS,)),
             pltpu.SemaphoreType.DMA((2,)),
-            pltpu.SemaphoreType.DMA((8,)),
-            pltpu.SemaphoreType.DMA((8,)),
+            pltpu.SemaphoreType.DMA((6,)),
+            pltpu.SemaphoreType.DMA((6,)),
         ],
         compiler_params=pltpu.CompilerParams(
             collective_id=0, has_side_effects=True, vmem_limit_bytes=56 * 1024 * 1024

time: 59.3 us -> 57.4 us (0.968)
  Pallas kernels: 58.2 us -> 56.5 us
    pallas_call x1, Pallas kernels: 58.2 us -> 56.5 us  [local(): pl.pallas_call(kernel, out_shape=pltpu.VMEM((w_out.shape[1], n_grid), BF)...]
where the time goes in v5:
time: 57.4 us; the launch traced here: 57.2 us
  Pallas kernels  56.5 us (98%)
  local copies, waits for them, and re-layouts  0.78 us (1%)
    pallas_call x1, Pallas kernels, local(): pl.pallas_call(kernel, out_shape=pltpu.VMEM((w_out.shape[1], n_grid), BF)...  56.5 us

profile of v5, /device:TPU:56, one launch (start us, length us, event | category | flops | bytes accessed | tf_op | source)
XLA Modules:
  0.0 57.2 jit_solution(10558984382171459158)
XLA Ops:
  0.0 56.5 %graph_weather.1 = bf16[227,1024]{1,0:T(8,128)(2,1)S(1)} custom-call(s32[16,32]{1,0:T(8,128)} %bitcast.18, s32[8,32]{1,0:T(8,128)} %bitcast.21, s32[8,32]{1,0:T(8,128)} %bitcast.22, bf16[227,1024]{1,0:T(8,128)(2,1)} %bitcast.14, bf16[227,512]{1,0:T(8,128)(2,1)} %refs_4_.1, bf16[512,512]{1,0:T(8,128)(2,1)} %refs_5_.1, s32[1,2048]{1,0:T(1,128)} %bitcast.19, ...), custom_call_target="tpu_custom_call" | custom-call | tf_op jit(solution)/shard_map/graph_weather/pallas_call | solution.py:551
  56.5 0.8 %copy.26 = bf16[1024,227]{0,1:T(8,128)(2,1)} copy(bf16[1024,227]{0,1:T(8,128)(2,1)S(1)} %bitcast.13) | data formatting | bytes 929792

commit v6 on v5

--- a/solution.py
+++ b/solution.py
@@ -200,13 +200,14 @@
     grid_turned[:, 0:channels] = jnp.transpose(grid_in[...])
 
     def embed(i, carry):
-        part = pl.ds(pl.multiple_of(i * 512, 512), 512)
+        part = pl.ds(i * 512, 512)
         latent = silu(dot(grid_turned[part, 0:channels], w_embed[...])).astype(BF)
         grid_latent[part, :] = latent
         enc_table[part, :] = dot(latent, w_grid_send[...]).astype(BF)
         return carry
 
-    lax.fori_loop(0, n_grid // 512, embed, 0)
+    for i in range(n_grid // 512):
+        embed(i, 0)
 
     def edge_rows(scratch, feat, sender, n_local, n_slots):
         value = sender[...]
@@ -222,7 +223,7 @@
         scratch[4:5, :] = jnp.where(local, value, -1).astype(F32)
         scratch[5:6, :] = jnp.where(local, -1, lent).astype(F32)
 
-    def sender_hot(scratch, hots, n_local, n_lent):
+    def sender_hot(scratch, hots, n_local, n_lent, first=0, last=None):
         def step(i, carry):
             part = pl.ds(pl.multiple_of(i * 128, 128), 128)
             turned = jnp.transpose(
@@ -238,7 +239,8 @@
                 hots[part, at : at + 128] = hot(lent, 128.0 * j, 0.5)
             return carry
 
-        lax.fori_loop(0, hots.shape[0] // 128, step, 0, unroll=8)
+        last = hots.shape[0] // 128 if last is None else last
+        lax.fori_loop(first, last, step, 0, unroll=8)
 
     def receiver_hot(target, hots, count):
         n_rows = hots.shape[0]
@@ -267,7 +269,7 @@
     for load in loads[6:10]:
         load.wait()
     edge_rows(enc_rows, enc_feat, enc_sender, n_grid, SLOTS_GRID)
-    sender_hot(enc_rows, enc_hot, n_grid, N_DOM * SLOTS_GRID)
+    sender_hot(enc_rows, enc_hot, n_grid, N_DOM * SLOTS_GRID, 0, 8)
     edge_weights(enc_table, n_grid, w_enc_edge[...])
 
     def ship(x, h):
@@ -307,13 +309,14 @@
         rows_out[0, h] = lent.reshape(16 * N_DOM, quarter).astype(BF)
         ship(0, h)
 
-    for q in range(N_DOM):
-        for lent, first in ((lend_mesh, 16), (lend_dec, 24)):
+    def mesh_lend(k, lent, first):
+        for q in range(N_DOM):
             column = jnp.broadcast_to(listed[first : first + 8, q : q + 1], (8, 128))
             lent[16 * q : 16 * q + 8, :] = column
             lent[16 * q + 8 : 16 * q + 16, :] = column + 128.0
-    for k, lent in enumerate((lend_mesh, lend_dec)):
         lend_hot[k] = jnp.concatenate([hot(lent[...], 0.0), hot(lent[...], 128.0)], axis=1)
+
+    mesh_lend(0, lend_mesh, 16)
 
     def local_sums(hots, columns, table):
         def step(i, carry):
@@ -323,6 +326,7 @@
 
         lax.fori_loop(0, hots.shape[0] // 1024, step, 0)
 
+    sender_hot(enc_rows, enc_hot, n_grid, N_DOM * SLOTS_GRID, 8, 16)
     local_sums(enc_hot, near, enc_table[...])
     receiver_hot(enc_offset, enc_to, enc_count)
 
@@ -446,6 +450,7 @@
             edge_rows(dec_rows, dec_feat, dec_sender, n_mesh, SLOTS_MESH)
             sender_hot(dec_rows, dec_hot, n_mesh, N_DOM * SLOTS_MESH)
             dec_receivers()
+            mesh_lend(1, lend_dec, 24)
         wait_for(wide_got.at[k, pl.ds(16, 16 * (N_DOM - 1))], recv_sem.at[2 + k])
         total = edge_sum[0 : mesh_hot.shape[0], :] + dot(mesh_hot[:, 256:512], beside(wide_got[k]))
         message = silu_of_half(total).astype(BF)
@@ -472,11 +477,13 @@
             grid_mean[128 * g : 128 * g + 128, :] = (
                 running[last[g], :, at : at + half] * jnp.concatenate([count] * (half // 128), axis=1)
             ).astype(BF)
-        total = mixed[...] + dot(grid_mean[...], w_dec[at : at + half, :])
-        if h == 0:
-            mixed[...] = total
-        else:
-            out[...] = dot_turned(w_out[...], silu(total).astype(BF)).astype(BF)
+        for i in range(n_grid // 512):
+            part = pl.ds(512 * i, 512)
+            total = mixed[part, :] + dot(grid_mean[part, :], w_dec[at : at + half, :])
+            if h == 0:
+                mixed[part, :] = total
+            else:
+                out[:, part] = dot_turned(w_out[...], silu(total).astype(BF)).astype(BF)
 
     wait_for(lists_got.at[pl.ds(1, N_DOM - 1)], lists_sem.at[0])
     for x in range(2):

time: 57.4 us -> 56.4 us (0.983)
  Pallas kernels: 56.5 us -> 55.4 us
    pallas_call x1, Pallas kernels: 56.5 us -> 55.4 us  [local(): pl.pallas_call(kernel, out_shape=pltpu.VMEM((w_out.shape[1], n_grid), BF)...]
where the time goes in v6:
time: 56.4 us; the launch traced here: 56.2 us
  Pallas kernels  55.4 us (98%)
  local copies, waits for them, and re-layouts  0.78 us (1%)
    pallas_call x1, Pallas kernels, local(): pl.pallas_call(kernel, out_shape=pltpu.VMEM((w_out.shape[1], n_grid), BF)...  55.4 us

profile of v6, /device:TPU:56, one launch (start us, length us, event | category | flops | bytes accessed | tf_op | source)
XLA Modules:
  0.0 56.2 jit_solution(1025560678101294083)
XLA Ops:
  0.0 55.4 %graph_weather.1 = bf16[227,1024]{1,0:T(8,128)(2,1)S(1)} custom-call(s32[16,32]{1,0:T(8,128)} %bitcast.18, s32[8,32]{1,0:T(8,128)} %bitcast.21, s32[8,32]{1,0:T(8,128)} %bitcast.22, bf16[227,1024]{1,0:T(8,128)(2,1)} %bitcast.14, bf16[227,512]{1,0:T(8,128)(2,1)} %refs_4_.1, bf16[512,512]{1,0:T(8,128)(2,1)} %refs_5_.1, s32[1,2048]{1,0:T(1,128)} %bitcast.19, ...), custom_call_target="tpu_custom_call" | custom-call | tf_op jit(solution)/shard_map/graph_weather/pallas_call | solution.py:558
  55.4 0.8 %copy.26 = bf16[1024,227]{0,1:T(8,128)(2,1)} copy(bf16[1024,227]{0,1:T(8,128)(2,1)S(1)} %bitcast.13) | data formatting | bytes 929792

commit v7 on v6

--- a/solution.py
+++ b/solution.py
@@ -319,12 +319,9 @@
     mesh_lend(0, lend_mesh, 16)
 
     def local_sums(hots, columns, table):
-        def step(i, carry):
-            part = pl.ds(pl.multiple_of(i * 1024, 1024), 1024)
+        for i in range(hots.shape[0] // 1024):
+            part = pl.ds(i * 1024, 1024)
             edge_sum[part, :] = dot(hots[part, 0:columns], table)
-            return carry
-
-        lax.fori_loop(0, hots.shape[0] // 1024, step, 0)
 
     sender_hot(enc_rows, enc_hot, n_grid, N_DOM * SLOTS_GRID, 8, 16)
     local_sums(enc_hot, near, enc_table[...])

time: 56.4 us -> 57.3 us (1.016)
  Pallas kernels: 55.4 us -> 56.3 us
    pallas_call x1, Pallas kernels: 55.4 us -> 56.3 us  [local(): pl.pallas_call(kernel, out_shape=pltpu.VMEM((w_out.shape[1], n_grid), BF)...]
where the time goes in v7:
time: 57.3 us; the launch traced here: 57.1 us
  Pallas kernels  56.3 us (98%)
  local copies, waits for them, and re-layouts  0.78 us (1%)
    pallas_call x1, Pallas kernels, local(): pl.pallas_call(kernel, out_shape=pltpu.VMEM((w_out.shape[1], n_grid), BF)...  56.3 us

profile of v7, /device:TPU:56, one launch (start us, length us, event | category | flops | bytes accessed | tf_op | source)
XLA Modules:
  0.0 57.1 jit_solution(8582523700253357474)
XLA Ops:
  0.0 56.3 %graph_weather.1 = bf16[227,1024]{1,0:T(8,128)(2,1)S(1)} custom-call(s32[16,32]{1,0:T(8,128)} %bitcast.18, s32[8,32]{1,0:T(8,128)} %bitcast.21, s32[8,32]{1,0:T(8,128)} %bitcast.22, bf16[227,1024]{1,0:T(8,128)(2,1)} %bitcast.14, bf16[227,512]{1,0:T(8,128)(2,1)} %refs_4_.1, bf16[512,512]{1,0:T(8,128)(2,1)} %refs_5_.1, s32[1,2048]{1,0:T(1,128)} %bitcast.19, ...), custom_call_target="tpu_custom_call" | custom-call | tf_op jit(solution)/shard_map/graph_weather/pallas_call | solution.py:555
  56.3 0.8 %copy.26 = bf16[1024,227]{0,1:T(8,128)(2,1)} copy(bf16[1024,227]{0,1:T(8,128)(2,1)S(1)} %bitcast.13) | data formatting | bytes 929792
